TPU v7x, 128 devices: a whole 4x4x4 slice. The times are simulated.
128 devices in a mesh: dp: 64 (over x, z, y), tensor: 2 (over core).
Axes of the slice: x: 4, y: 4, z: 4, core: 2. Of those that a mesh axis runs over, the one named last changes fastest.
Arguments:
- latent_kv: bfloat16 [32768, 512], P('dp', 'tensor'), may hold values from -6 to 6
- latent_q: bfloat16 [32768, 1536], P('dp', 'tensor'), may hold values from -6 to 6
- grad_kv: bfloat16 [32768, 8192], P('dp'), may hold values from -0.09375 to 0.09375
- grad_q: bfloat16 [32768, 6144], P('dp'), may hold values from -0.09375 to 0.09375
- momentum_kv: float32 [8192, 512], P('dp', 'tensor'), may hold values from -20 to 20
- momentum_q: float32 [6144, 1536], P('dp', 'tensor'), may hold values from -20 to 20
Outputs:
- update_kv: bfloat16 [8192, 512], P('dp', 'tensor')
- momentum_kv_new: float32 [8192, 512], P('dp', 'tensor')
- update_q: bfloat16 [6144, 1536], P('dp', 'tensor')
- momentum_q_new: float32 [6144, 1536], P('dp', 'tensor')
All inputs are finite; a program needn't handle non-finite values.
Results may differ from a plain program's by a relative error of at most 0.035.
Values may be sent and summed in bfloat16 or wider, within the bound.
A program may use at most 256 MiB of HBM per device.

v0:
```python
import jax
import jax.numpy as jnp
from jax import lax
from jax.sharding import PartitionSpec as P

ITERS = 5


first_coef = 3.4445
second_coef = -4.775
third_coef = 2.0315
momentum_rate = 0.95
norm_eps = 1e-07


def from_partner(shard, axis, bit):
    return lax.ppermute(shard, axis, [(i, i ^ 1 << bit) for i in range(lax.axis_size(axis))])


def half_terms(grads, latents):
    return lax.dot_general(
        grads, latents, (((0,), (0,)), ((), ())), preferred_element_type=jnp.float32
    )


def place_pair(mine, theirs, parity, along):
    return jnp.where(
        parity == 0, jnp.concatenate([mine, theirs], along), jnp.concatenate([theirs, mine], along)
    )


def outer_self(matrix):
    return lax.dot_general(
        matrix, matrix, (((1,), (1,)), ((), ())), preferred_element_type=jnp.float32
    )


def mixer(gram_sum):
    gram_low = gram_sum.astype(jnp.bfloat16)
    square = jnp.dot(gram_low, gram_low, preferred_element_type=jnp.float32)
    return (second_coef * gram_low.astype(jnp.float32) + third_coef * square).astype(jnp.bfloat16)


def advance(iterate, mixing, source):
    moved = jnp.dot(mixing, source, preferred_element_type=jnp.float32)
    return (first_coef * iterate.astype(jnp.float32) + moved).astype(jnp.bfloat16)


def split_rows(prepared_kv, prepared_q, parity):
    squares = lax.psum(
        (jnp.sum(prepared_kv * prepared_kv), jnp.sum(prepared_q * prepared_q)), "tensor"
    )
    partner = from_partner((squares[0], squares[1]), "dp", 0)
    iterates = []
    for prepared, own_square, far_square in zip((prepared_kv, prepared_q), squares, partner):
        iterates.append(
            (prepared / (jnp.sqrt(own_square + far_square) + norm_eps)).astype(jnp.bfloat16)
        )
    for sweep in range(ITERS):
        arrived = from_partner((iterates[0], iterates[1]), "dp", 0)
        stacked = [place_pair(mine, theirs, parity, 0) for mine, theirs in zip(iterates, arrived)]
        grams = lax.psum((outer_self(stacked[0]), outer_self(stacked[1])), "tensor")
        renewed = []
        for mine, whole_rows, gram_sum in zip(iterates, stacked, grams):
            mixing = mixer(gram_sum)
            half_rows = mine.shape[0]
            own_mix = lax.dynamic_slice_in_dim(mixing, parity * half_rows, half_rows, 0)
            renewed.append(advance(mine, own_mix, whole_rows))
        iterates = renewed
    return iterates


def prepare(held_kv, held_q, gradient_kv, gradient_q):
    renewed_kv = momentum_rate * held_kv + gradient_kv
    renewed_q = momentum_rate * held_q + gradient_q
    prepared_kv = gradient_kv + momentum_rate * renewed_kv
    prepared_q = gradient_q + momentum_rate * renewed_q
    return (renewed_kv, renewed_q, prepared_kv, prepared_q)


def per_device(latent_kv, latent_q, grad_kv, grad_q, momentum_kv, momentum_q):
    parity = lax.axis_index("dp") % 2
    gradient_kv = lax.psum_scatter(
        half_terms(grad_kv, latent_kv), "dp", scatter_dimension=0, tiled=True
    )
    gradient_q = lax.psum_scatter(
        half_terms(grad_q, latent_q), "dp", scatter_dimension=0, tiled=True
    )
    renewed_kv, renewed_q, prepared_kv, prepared_q = prepare(
        momentum_kv, momentum_q, gradient_kv, gradient_q
    )
    iterates = split_rows(prepared_kv, prepared_q, parity)
    return (iterates[0], renewed_kv, iterates[1], renewed_q)


def solution(mesh):
    in_specs = (
        P("dp", "tensor"),
        P("dp", "tensor"),
        P("dp", None),
        P("dp", None),
        P("dp", "tensor"),
        P("dp", "tensor"),
    )
    out_specs = (P("dp", "tensor"), P("dp", "tensor"), P("dp", "tensor"), P("dp", "tensor"))
    return jax.shard_map(
        per_device, mesh=mesh, in_specs=in_specs, out_specs=out_specs, check_vma=False
    )
```

profile of v0, /device:TPU:1, one launch (start us, length us, event | category | flops | bytes accessed | tf_op | source)
XLA Modules:
  0.0 711.7 jit_solution(11164826834860588452)
XLA Ops:
  7.2 9.2 %fusion.130 = f32[8192,256]{1,0:T(8,128)} fusion(bf16[512,8192]{1,0:T(8,128)(2,1)} %param.8, bf16[512,256]{1,0:T(8,128)(2,1)} %param.6), kind=kOutput, calls=%fused_computation.158 | convolution fusion | flops 2147483648 | bytes 17039360 | tf_op jit(solution)/shard_map/dot_general | solution.py:21
  16.5 11.9 %fusion.136 = f32[6144,768]{1,0:T(8,128)} fusion(bf16[512,6144]{1,0:T(8,128)(2,1)} %param.9, bf16[512,768]{1,0:T(8,128)(2,1)S(1)} %copy-done), kind=kOutput, calls=%fused_computation.164 | convolution fusion | flops 4831838208 | bytes 25952256 | tf_op jit(solution)/shard_map/dot_general | solution.py:21
  28.4 311.4 %reduce-scatter.3.cloned.1.call-done = f32[128,256]{1,0:T(8,128)} async-done(((f32[8192,256]{1,0:T(8,128)}), f32[128,256]{1,0:T(8,128)}) %reduce-scatter.3.cloned.1.call-update) | async-done | bytes 131088 | tf_op jit(solution)/shard_map/reduce_scatter | solution.py:83
  339.8 1.5 multiply_reduce_fusion.1
  341.3 282.3 %reduce-scatter.5.cloned.1.call-done = f32[96,768]{1,0:T(8,128)} async-done(((f32[6144,768]{1,0:T(8,128)}), f32[96,768]{1,0:T(8,128)}) %reduce-scatter.5.cloned.1.call-update) | async-done | bytes 294928 | tf_op jit(solution)/shard_map/reduce_scatter | solution.py:86
  623.6 1.6 multiply_reduce_fusion
  625.3 5.3 all-reduce.5
  630.7 1.4 collective-permute-start
  632.1 1.2 collective-permute-done.6
  635.9 0.9 divide_convert_fusion.1
  637.0 1.0 divide_convert_fusion
  638.0 1.5 collective-permute-start.7
  640.3 2.5 collective-permute-done.7
  643.1 7.1 all-reduce.11
  650.7 1.0 collective-permute-start.2
  652.6 1.8 collective-permute-done.2
  654.6 2.8 collective-permute-done.8
  657.7 5.7 all-reduce.12
  663.9 1.0 collective-permute-start.3
  665.7 1.8 collective-permute-done.3
  667.7 2.8 collective-permute-done.9
  670.8 5.6 all-reduce.13
  677.0 1.0 collective-permute-start.4
  678.9 1.8 collective-permute-done.4
  680.9 2.8 collective-permute-done.10
  684.0 5.7 all-reduce.14
  690.2 1.0 collective-permute-start.5
  692.0 1.8 collective-permute-done.5
  694.0 2.8 collective-permute-done.11
  697.1 5.6 all-reduce.15
  703.1 0.9 fusion.4
  704.0 0.8 fusion.9
  (50 shorter events, 9.3 us)
Async XLA Ops:
  7.2 9.3 %copy-start = (bf16[512,768]{1,0:T(8,128)(2,1)S(1)}, bf16[512,768]{1,0:T(8,128)(2,1)}, u32[]{:S(2)}) copy-start(bf16[512,768]{1,0:T(8,128)(2,1)} %param.7) | copy-start | bytes 2359300
  7.2 332.6 %reduce-scatter.3.cloned.1.call-start = ((), (), s32[]{:S(2)}) async-start(), calls=%async_computation.2 | async-start | bytes 8519680 | tf_op jit(solution)/shard_map/reduce_scatter | solution.py:83
  16.4 607.2 %reduce-scatter.5.cloned.1.call-start = ((), (), s32[]{:S(2)}) async-start(), calls=%async_computation.3 | async-start | bytes 19169280 | tf_op jit(solution)/shard_map/reduce_scatter | solution.py:86
  28.4 311.4 %copy-start.4 = (f32[128,256]{1,0:T(8,128)S(1)}, f32[128,256]{1,0:T(8,128)}, u32[]{:S(2)}) copy-start(f32[128,256]{1,0:T(8,128)} %param.10) | copy-start | bytes 393220
  28.4 595.3 %copy-start.3 = (f32[96,768]{1,0:T(8,128)S(1)}, f32[96,768]{1,0:T(8,128)}, u32[]{:S(2)}) copy-start(f32[96,768]{1,0:T(8,128)} %param.11) | copy-start | bytes 884740
  341.3 335.7 %copy-start.2 = (f32[128,256]{1,0:T(8,128)}, f32[128,256]{1,0:T(8,128)S(1)}, u32[]{:S(2)}) copy-start(f32[128,256]{1,0:T(8,128)S(1)} %get-tuple-element.19) | copy-start | bytes 393220
  625.3 53.0 %copy-start.1 = (f32[96,768]{1,0:T(8,128)}, f32[96,768]{1,0:T(8,128)S(1)}, u32[]{:S(2)}) copy-start(f32[96,768]{1,0:T(8,128)S(1)} %get-tuple-element.17) | copy-start | bytes 884740
  630.6 2.6 collective-permute-start.6
  630.7 3.9 collective-permute-start
  636.8 3.2 collective-permute-start.1
  638.0 4.8 collective-permute-start.7
  650.7 3.6 collective-permute-start.2
  652.0 5.4 collective-permute-start.8
  663.9 3.6 collective-permute-start.3
  665.1 5.4 collective-permute-start.9
  677.0 3.6 collective-permute-start.4
  678.3 5.4 collective-permute-start.10
  690.2 3.6 collective-permute-start.5
  691.4 5.4 collective-permute-start.11
Sparse Core Ops, SparseCore 0:
  16.6 323.1 reduce-scatter.2
  344.5 279.0 reduce-scatter.4
where the time goes:
time: 712 us
  waiting for transfers between devices  616 us (87%)
  blocking collectives  35.1 us (5%)
  matrix products  28.6 us (4%)
  between operations  16.9 us (2%)
  starting transfers between devices  9.66 us (1%)
    reduce_scatter x1, waiting for transfers between devices, per_device(): lax.psum_scatter(half_terms(grad_kv, latent_kv), 'dp', scatter_dimension=...  311 us
    reduce_scatter x1, waiting for transfers between devices, per_device(): lax.psum_scatter(half_terms(grad_q, latent_q), 'dp', scatter_dimension=0,...  282 us
    psum x5, blocking collectives, split_rows(): grams = lax.psum((outer_self(stacked[0]), outer_self(stacked[1])), 'tensor')  29.7 us
    ppermute x12, waiting for transfers between devices, from_partner(): lax.ppermute(shard, axis, [(i, i ^ 1 << bit) for i in range(lax.axis_size...  22.6 us
    dot_general x2, matrix products, half_terms(): lax.dot_general(grads, latents, (((0,), (0,)), ((), ())), preferred_eleme...  21.1 us
  transfers between devices with their start and end apart: 14, of which 13 were waited for; matrix products, arithmetic and copies ran while one was open for 2% of the time, Pallas kernels for 0%

commit v1 on v0

v1 whole, which is shorter than its diff:
```python
import functools

import jax
import jax.numpy as jnp
from jax import lax
from jax.experimental import pallas as pl
from jax.experimental.pallas import tpu as pltpu
from jax.sharding import PartitionSpec as P

ITERS = 5
SIDE = 4
MESH = pl.DeviceIdType.MESH

first_coef = 3.4445
second_coef = -4.775
third_coef = 2.0315
momentum_rate = 0.95
norm_eps = 1e-07

TOK = 512
KV_ROWS, KV_COLS = 128, 256
Q_ROWS, Q_COLS = 96, 768
KV_CUT = ((0, 48), (48, 48), (96, 32))
SLAB = 256
ORDERS = ("xzy", "zyx", "yxz")


def shifted(where, axis, step):
    moved = dict(where)
    moved[axis] = lax.rem(moved[axis] + step + SIDE, SIDE)
    return (moved["x"] * SIDE + moved["z"]) * SIDE + moved["y"]


def gram_of(matrix):
    return lax.dot_general(
        matrix, matrix, (((1,), (1,)), ((), ())), preferred_element_type=jnp.float32
    )


def mixer(matrix):
    gram_low = gram_of(matrix).astype(jnp.bfloat16)
    square = jnp.dot(gram_low, gram_low, preferred_element_type=jnp.float32)
    return (second_coef * gram_low.astype(jnp.float32) + third_coef * square).astype(jnp.bfloat16)


def advance(iterate, mixing, source):
    moved = jnp.dot(mixing, source, preferred_element_type=jnp.float32)
    return (first_coef * iterate.astype(jnp.float32) + moved).astype(jnp.bfloat16)


def add_into(target, others, count):
    def step(i, carry):
        total = target[i].astype(jnp.float32)
        for other in others:
            total += other[i].astype(jnp.float32)
        target[i] = total.astype(target.dtype)
        return carry

    lax.fori_loop(0, count, step, 0)


def kernel(
    lat_kv, lat_q, grad_kv, grad_q, mom_kv, mom_q,
    up_kv, new_kv, up_q, new_q,
    lk, lq, gk, gq, part_k, part_q, one_k, one_q, two_k, two_q, three_k, three_q,
    sum_k, sum_q, x_k, x_q, mix_k, mix_q,
    in_sem, gk_sem, gq_sem, send_sem, recv_sem, ag_send, ag_recv,
):
    me = lax.axis_index("dp")
    core = lax.axis_index("tensor")
    where = {"x": me // 16, "z": lax.rem(me // 4, 4), "y": lax.rem(me, 4)}
    low = lax.rem(me, 2)
    twin = me + 1 - 2 * low
    group = ((me, 1 - core), (twin, core), (twin, 1 - core))

    def unit(xr, zr):
        return lax.rem(where["x"] + xr, 4) * 4 + lax.rem(where["z"] + zr, 4)

    def fetch(source, target, sems, width, i):
        at = pl.multiple_of(unit(i // 4, lax.rem(i, 4)) * width, 128)
        return pltpu.make_async_copy(source.at[:, pl.ds(at, width)], target.at[i], sems.at[i])

    fetch_q = functools.partial(fetch, grad_q, gq, gq_sem, 4 * Q_ROWS)
    fetch_k = functools.partial(fetch, grad_kv, gk, gk_sem, 4 * KV_ROWS)
    load_lq = pltpu.make_async_copy(lat_q, lq, in_sem.at[0])
    load_lk = pltpu.make_async_copy(lat_kv, lk, in_sem.at[1])
    load_lq.start()

    def begin(which, i, carry):
        which(i).start()
        return carry

    for row in (2, 3, 1, 0):
        lax.fori_loop(row * 4, row * 4 + 4, functools.partial(begin, fetch_q), 0)
    load_lk.start()
    for row in (2, 3, 1, 0):
        lax.fori_loop(row * 4, row * 4 + 4, functools.partial(begin, fetch_k), 0)

    barrier = pltpu.get_barrier_semaphore()
    friends = [(shifted(where, a, s), core) for a in "xyz" for s in (1, 2, 3)]
    friends += [group[0], group[2]]
    for friend in friends:
        pl.semaphore_signal(barrier, inc=1, device_id=friend, device_id_type=MESH)
    pl.semaphore_wait(barrier, len(friends))

    started = []

    def send(chunk, s, slot, source, target, axis, step):
        copy = pltpu.make_async_remote_copy(
            src_ref=source,
            dst_ref=target,
            send_sem=send_sem.at[chunk, s, slot],
            recv_sem=recv_sem.at[chunk, s, slot],
            device_id=(shifted(where, axis, step), core),
            device_id_type=MESH,
        )
        copy.start()
        started.append(copy)
        return copy

    class Chunk:
        def __init__(self, index, parts, ones, twos, threes):
            self.index, self.parts, self.ones = index, parts, ones
            self.twos, self.threes = twos, threes
            self.copies = {}

        def go(self, s, slot, source, target, axis, step):
            self.copies[s, slot] = send(self.index, s, slot, source, target, axis, step)

        def one_far(self, s):
            part, got, axis = self.parts[s], self.ones[s], ORDERS[s][0]
            self.go(s, 0, part.at[2, pl.ds(0, 2)], got.at[0], axis, 1)
            self.go(s, 1, part.at[2, pl.ds(2, 2)], got.at[1], axis, -1)

        def one_up(self, s):
            part, got, axis = self.parts[s], self.ones[s], ORDERS[s][0]
            self.go(s, 2, part.at[1, pl.ds(2, 2)], got.at[2], axis, 1)

        def one_down(self, s):
            part, got, axis = self.parts[s], self.ones[s], ORDERS[s][0]
            self.go(s, 3, part.at[3, pl.ds(0, 2)], got.at[3], axis, -1)

        def one_relay(self, s):
            part, got, axis = self.parts[s], self.ones[s], ORDERS[s][0]
            self.copies[s, 0].wait_recv()
            for b in range(2):
                add_into(part.at[1, b], [got.at[0, b]], 4)
            self.go(s, 4, part.at[1, pl.ds(0, 2)], got.at[4], axis, 1)
            self.copies[s, 1].wait_recv()
            for b in range(2):
                add_into(part.at[3, 2 + b], [got.at[1, b]], 4)
            self.go(s, 5, part.at[3, pl.ds(2, 2)], got.at[5], axis, -1)

        def one_end_two_begin(self, s):
            part, got, axis = self.parts[s], self.ones[s], ORDERS[s][1]
            two = self.twos[s]
            self.copies[s, 2].wait_recv()
            self.copies[s, 5].wait_recv()
            for b in (2, 3):
                add_into(part.at[0, b], [got.at[2, b - 2], got.at[5, b - 2]], 4)
                self.go(s, 4 + b, part.at[0, b], two.at[b - 1], axis, b)
            self.copies[s, 3].wait_recv()
            self.copies[s, 4].wait_recv()
            for b in (1, 0):
                add_into(part.at[0, b], [got.at[3, b], got.at[4, b]], 4)
                if b == 1:
                    self.go(s, 8, part.at[0, 1], two.at[0], axis, 1)

        def two_end_three_begin(self, s):
            part, two, three = self.parts[s], self.twos[s], self.threes[s]
            for slot in (6, 7, 8):
                self.copies[s, slot].wait_recv()
            add_into(part.at[0, 0], [two.at[0], two.at[1], two.at[2]], 4)
            for c in (1, 2, 3):
                self.go(s, 8 + c, part.at[0, 0, c], three.at[c - 1], ORDERS[s][2], c)

        def three_end(self, s):
            part, three = self.parts[s], self.threes[s]
            for slot in (9, 10, 11):
                self.copies[s, slot].wait_recv()
            total = part[0, 0, 0].astype(jnp.float32)
            for c in range(3):
                total += three[c].astype(jnp.float32)
            return total

    chunk_q = Chunk(0, part_q, one_q, two_q, three_q)
    chunk_k = Chunk(1, part_k, one_k, two_k, three_k)

    def place_of(xr, zr, yr):
        at = {"x": xr, "z": zr, "y": yr}
        return [tuple(at[a] for a in order) for order in ORDERS]

    def unit_q(i, carry):
        fetch_q(i).wait()
        xr, zr = i // 4, lax.rem(i, 4)
        term = lax.dot_general(
            gq[i], lq[...], (((0,), (0,)), ((), ())), preferred_element_type=jnp.float32
        ).astype(jnp.bfloat16)
        for y in range(4):
            yr = lax.rem(y - where["y"] + 4, 4)
            for s, place in enumerate(place_of(xr, zr, yr)):
                part_q[s][place] = term[y * Q_ROWS:(y + 1) * Q_ROWS, s * SLAB:(s + 1) * SLAB]
        return carry

    def unit_k(i, carry):
        fetch_k(i).wait()
        xr, zr = i // 4, lax.rem(i, 4)
        term = lax.dot_general(
            gk[i], lk[...], (((0,), (0,)), ((), ())), preferred_element_type=jnp.float32
        ).astype(jnp.bfloat16)
        for y in range(4):
            yr = lax.rem(y - where["y"] + 4, 4)
            for s, place in enumerate(place_of(xr, zr, yr)):
                at, rows = KV_CUT[s]
                part_k[s][place] = term[y * KV_ROWS + at:y * KV_ROWS + at + rows]
        return carry

    load_lq.wait()
    lax.fori_loop(8, 12, unit_q, 0)
    chunk_q.one_far(0)
    lax.fori_loop(12, 16, unit_q, 0)
    chunk_q.one_down(0)
    lax.fori_loop(4, 8, unit_q, 0)
    chunk_q.one_up(0)
    lax.fori_loop(0, 4, unit_q, 0)
    for s in (1, 2):
        chunk_q.one_far(s)
        chunk_q.one_down(s)
        chunk_q.one_up(s)

    load_lk.wait()
    lax.fori_loop(0, 16, unit_k, 0)

    for s in range(3):
        chunk_q.one_relay(s)
    for s in range(3):
        chunk_k.one_far(s)
        chunk_k.one_down(s)
        chunk_k.one_up(s)
    for s in range(3):
        chunk_q.one_end_two_begin(s)
    for s in range(3):
        chunk_k.one_relay(s)
    for s in range(3):
        chunk_q.two_end_three_begin(s)
    for s in range(3):
        chunk_k.one_end_two_begin(s)

    def gather(chunk, x_ref, rows, cols):
        def slot(owner, c):
            return x_ref.at[
                pl.ds(pl.multiple_of(lax.rem(owner, 2) * rows, rows), rows),
                pl.ds(pl.multiple_of(c * cols, cols), cols),
            ]

        mine = slot(me, core)
        copies = []
        for k, (owner, c) in enumerate(group):
            copies.append(
                pltpu.make_async_remote_copy(
                    src_ref=mine,
                    dst_ref=mine,
                    send_sem=ag_send.at[chunk, k],
                    recv_sem=ag_recv.at[chunk, k],
                    device_id=(owner, c),
                    device_id_type=MESH,
                )
            )
            copies[-1].start()

        def finish():
            for k, (owner, c) in enumerate(group):
                pltpu.make_async_remote_copy(
                    src_ref=mine,
                    dst_ref=slot(owner, c),
                    send_sem=ag_send.at[chunk, k],
                    recv_sem=ag_recv.at[chunk, k],
                    device_id=(owner, c),
                    device_id_type=MESH,
                ).wait_recv()
            for copy in copies:
                copy.wait_send()

        return finish

    def own_rows(rows):
        return pl.ds(pl.multiple_of(low * rows, rows), rows)

    def own_cols(cols):
        return pl.ds(pl.multiple_of(core * cols, cols), cols)

    def prepare(gradient, held, new_ref, x_ref, rows, cols):
        renewed = momentum_rate * held[...] + gradient
        new_ref[...] = renewed
        prepared = gradient + momentum_rate * renewed
        x_ref[own_rows(rows), own_cols(cols)] = prepared.astype(jnp.bfloat16)

    def newton(x_ref, mix_ref, out_ref, rows, cols):
        wide = x_ref[...].astype(jnp.float32)
        norm = jnp.sqrt(jnp.sum(wide * wide, keepdims=True)) + norm_eps
        x_ref[...] = (wide / norm).astype(jnp.bfloat16)
        for sweep in range(ITERS - 1):
            whole = x_ref[...]
            x_ref[...] = advance(whole, mixer(whole), whole)
        mix_ref[...] = mixer(x_ref[...])
        out_ref[...] = advance(
            x_ref[own_rows(rows), own_cols(cols)],
            mix_ref[own_rows(rows), :],
            x_ref[:, own_cols(cols)],
        )

    for s in range(3):
        sum_q[:, s * SLAB:(s + 1) * SLAB] = chunk_q.three_end(s)
    prepare(sum_q[...], mom_q, new_q, x_q, Q_ROWS, Q_COLS)
    end_q = gather(0, x_q, Q_ROWS, Q_COLS)

    for s in range(3):
        chunk_k.two_end_three_begin(s)
    end_q()
    newton(x_q, mix_q, up_q, Q_ROWS, Q_COLS)

    for s in range(3):
        at, rows = KV_CUT[s]
        sum_k[at:at + rows, :] = chunk_k.three_end(s)
    prepare(sum_k[...], mom_kv, new_kv, x_k, KV_ROWS, KV_COLS)
    gather(1, x_k, KV_ROWS, KV_COLS)()
    newton(x_k, mix_k, up_kv, KV_ROWS, KV_COLS)

    for copy in started:
        copy.wait_send()


def per_device(latent_kv, latent_q, grad_kv, grad_q, momentum_kv, momentum_q):
    low, full = jnp.bfloat16, jnp.float32
    kv_rows = [rows for _, rows in KV_CUT]
    q_rows = [Q_ROWS] * 3

    def cells(lead, rows_of):
        return [pltpu.VMEM(lead + (rows, SLAB), low) for rows in rows_of]

    vmem = pl.BlockSpec(memory_space=pltpu.VMEM)
    hbm = pl.BlockSpec(memory_space=pl.ANY)
    return pl.pallas_call(
        kernel,
        out_shape=(
            jax.ShapeDtypeStruct((KV_ROWS, KV_COLS), low),
            jax.ShapeDtypeStruct((KV_ROWS, KV_COLS), full),
            jax.ShapeDtypeStruct((Q_ROWS, Q_COLS), low),
            jax.ShapeDtypeStruct((Q_ROWS, Q_COLS), full),
        ),
        in_specs=[hbm, hbm, hbm, hbm, vmem, vmem],
        out_specs=(vmem, vmem, vmem, vmem),
        scratch_shapes=[
            pltpu.VMEM((TOK, KV_COLS), low),
            pltpu.VMEM((TOK, Q_COLS), low),
            pltpu.VMEM((16, TOK, 4 * KV_ROWS), low),
            pltpu.VMEM((16, TOK, 4 * Q_ROWS), low),
            cells((4, 4, 4), kv_rows),
            cells((4, 4, 4), q_rows),
            cells((6, 2, 4), kv_rows),
            cells((6, 2, 4), q_rows),
            cells((3, 4), kv_rows),
            cells((3, 4), q_rows),
            cells((3,), kv_rows),
            cells((3,), q_rows),
            pltpu.VMEM((KV_ROWS, KV_COLS), full),
            pltpu.VMEM((Q_ROWS, Q_COLS), full),
            pltpu.VMEM((2 * KV_ROWS, 2 * KV_COLS), low),
            pltpu.VMEM((2 * Q_ROWS, 2 * Q_COLS), low),
            pltpu.VMEM((2 * KV_ROWS, 2 * KV_ROWS), low),
            pltpu.VMEM((2 * Q_ROWS, 2 * Q_ROWS), low),
            pltpu.SemaphoreType.DMA((2,)),
            pltpu.SemaphoreType.DMA((16,)),
            pltpu.SemaphoreType.DMA((16,)),
            pltpu.SemaphoreType.DMA((2, 3, 12)),
            pltpu.SemaphoreType.DMA((2, 3, 12)),
            pltpu.SemaphoreType.DMA((2, 3)),
            pltpu.SemaphoreType.DMA((2, 3)),
        ],
        compiler_params=pltpu.CompilerParams(
            collective_id=0, has_side_effects=True, vmem_limit_bytes=62 * 2**20
        ),
        name="muon",
    )(latent_kv, latent_q, grad_kv, grad_q, momentum_kv, momentum_q)


def solution(mesh):
    in_specs = (
        P("dp", "tensor"),
        P("dp", "tensor"),
        P("dp", None),
        P("dp", None),
        P("dp", "tensor"),
        P("dp", "tensor"),
    )
    out_specs = (P("dp", "tensor"), P("dp", "tensor"), P("dp", "tensor"), P("dp", "tensor"))
    return jax.shard_map(
        per_device, mesh=mesh, in_specs=in_specs, out_specs=out_specs, check_vma=False
    )
```

time: 712 us -> 97.2 us (0.14)
  waiting for transfers between devices: 616 us -> 0 us
  Pallas kernels: 0 us -> 90 us
  blocking collectives: 35.1 us -> 0 us
  matrix products: 28.6 us -> 0 us
  between operations: 16.9 us -> 0.64 us
  starting transfers between devices: 9.66 us -> 0 us
    reduce_scatter x2 -> x0, waiting for transfers between devices: 594 us -> none  [the longest x1 311 us: per_device(): lax.psum_scatter(half_terms(grad_kv, latent_kv), 'dp', scatter_dimension=...]
    pallas_call x0 -> x1, Pallas kernels: none -> 90 us  [per_device(): pl.pallas_call(kernel, out_shape=(jax.ShapeDtypeStruct((KV_ROWS, KV_COLS)...]
    psum x6 -> x0, blocking collectives: 35.1 us -> none  [the longest x5 29.7 us: split_rows(): grams = lax.psum((outer_self(stacked[0]), outer_self(stacked[1])), 'tensor')]
    dot_general x32 -> x0, matrix products: 28.6 us -> none  [the longest x2 21.1 us: half_terms(): lax.dot_general(grads, latents, (((0,), (0,)), ((), ())), preferred_eleme...]
    ppermute x12 -> x0, waiting for transfers between devices: 22.6 us -> none  [from_partner(): lax.ppermute(shard, axis, [(i, i ^ 1 << bit) for i in range(lax.axis_size...]
    ppermute x12 -> x0, starting transfers between devices: 9.58 us -> none  [from_partner(): lax.ppermute(shard, axis, [(i, i ^ 1 << bit) for i in range(lax.axis_size...]
  transfers between devices with their start and end apart: 14 -> 0, of which waited for: 13 -> 0; matrix products, arithmetic and copies ran while one was open for 2% -> 0% of each run, Pallas kernels for 0% -> 0%
where the time goes in v1:
time: 97.2 us; the launch traced here: 97 us
  Pallas kernels  90 us (93%)
  local copies, waits for them, and re-layouts  6.31 us (6%)
    pallas_call x1, Pallas kernels, per_device(): pl.pallas_call(kernel, out_shape=(jax.ShapeDtypeStruct((KV_ROWS, KV_COLS)...  90 us
    unnamed x4, local copies, waits for them, and re-layouts  6.31 us

profile of v1, /device:TPU:1, one launch (start us, length us, event | category | flops | bytes accessed | tf_op | source)
XLA Modules:
  0.0 97.0 jit_solution(14099567631099262095)
XLA Ops:
  0.6 90.0 %muon.1 = (bf16[128,256]{1,0:T(8,128)(2,1)}, f32[128,256]{1,0:T(8,128)}, bf16[96,768]{1,0:T(8,128)(2,1)}, f32[96,768]{1,0:T(8,128)}) custom-call(bf16[512,256]{1,0:T(8,128)(2,1)} %lat_kv.1, bf16[512,768]{1,0:T(8,128)(2,1)} %lat_q.1, bf16[512,8192]{1,0:T(8,128)(2,1)} %grad_kv.1, bf16[512,6144]{1,0:T(8,128)(2,1)} %grad_q.1, f32[128,256]{1,0:T(8,128)} %mom_kv.1, ...), custom_call_target="tpu_custom_call" | custom-call | tf_op jit(solution)/shard_map/muon/pallas_call | solution.py:343
  90.6 1.5 %copy.14 = bf16[128,256]{1,0:T(8,128)(2,1)} copy(bf16[128,256]{1,0:T(8,128)(2,1)} %get-tuple-element.8) | data formatting | bytes 131072
  92.1 1.6 %copy.15 = f32[128,256]{1,0:T(8,128)} copy(f32[128,256]{1,0:T(8,128)} %get-tuple-element.9) | data formatting | bytes 262144
  93.7 1.6 %copy.16 = bf16[96,768]{1,0:T(8,128)(2,1)} copy(bf16[96,768]{1,0:T(8,128)(2,1)} %get-tuple-element.10) | data formatting | bytes 294912
  95.3 1.7 %copy.17 = f32[96,768]{1,0:T(8,128)} copy(f32[96,768]{1,0:T(8,128)} %get-tuple-element.11) | data formatting | bytes 589824

commit v2 on v0

v2 whole, which is shorter than its diff:
```python
import functools

import jax
import jax.numpy as jnp
from jax import lax
from jax.experimental import pallas as pl
from jax.experimental.pallas import tpu as pltpu
from jax.sharding import PartitionSpec as P

ITERS = 5
SIDE = 4
MESH = pl.DeviceIdType.MESH

first_coef = 3.4445
second_coef = -4.775
third_coef = 2.0315
momentum_rate = 0.95
norm_eps = 1e-07

TOK = 512
KV_ROWS, KV_COLS = 128, 256
Q_ROWS, Q_COLS = 96, 768
LANES = 128
SLAB = 2 * LANES
ORDERS = ("xzy", "zyx", "yxz")
KV_CUT = ((0, 48), (48, 48), (96, 32))
Q_CUT = ((0, 96),) * 3
SECOND, THIRD, FOURTH = 6, 12, 15
SLOTS = 17
RINGS = ("q0", "q1")

PLAN = (
    "relay1 q0", "products k", "far k0", "far k1", "near k1", "second q0", "relay1 q1",
    "near k0", "relay1 k0", "relay2 q0", "relay1 k1", "second q1", "third q0", "relay2 q1",
    "second k0", "third q1", "second k1", "third k0", "last q1", "last q0", "gather q",
    "third k1", "last k0", "last k1", "gather k", "forward q", "end q", "end k",
)


def shifted(where, axis, step):
    moved = dict(where)
    moved[axis] = lax.rem(moved[axis] + step + SIDE, SIDE)
    return (moved["x"] * SIDE + moved["z"]) * SIDE + moved["y"]


def gram_of(matrix):
    return lax.dot_general(
        matrix, matrix, (((1,), (1,)), ((), ())), preferred_element_type=jnp.float32
    )


def mixers(grams):
    lows = [gram.astype(jnp.bfloat16) for gram in grams]
    squares = [jnp.dot(low, low, preferred_element_type=jnp.float32) for low in lows]
    return [
        (second_coef * low.astype(jnp.float32) + third_coef * square).astype(jnp.bfloat16)
        for low, square in zip(lows, squares)
    ]


def advance(iterate, mixing, source, scale=None):
    moved = jnp.dot(mixing, source, preferred_element_type=jnp.float32)
    total = first_coef * iterate.astype(jnp.float32) + moved
    if scale is not None:
        total = total * scale
    return total.astype(jnp.bfloat16)


def scale_of(gram):
    at = [lax.broadcasted_iota(jnp.int32, gram.shape, d) for d in range(2)]
    squares = jnp.sum(jnp.where(at[0] == at[1], gram, 0.0), keepdims=True)
    return 1.0 / (jnp.sqrt(squares) + norm_eps)


def newton(heads):
    own_row, own_col = lax.rem(lax.axis_index("dp"), 2), lax.axis_index("tensor")
    for sweep in range(ITERS):
        source = [head[0] if sweep == 0 else head[1] for head in heads]
        wholes = [ref[...] for ref in source]
        grams = [gram_of(whole) for whole in wholes]
        scales = [None] * len(heads)
        if sweep == 0:
            scales = [scale_of(gram) for gram in grams]
            grams = [gram * scale * scale for gram, scale in zip(grams, scales)]
        mixings = mixers(grams)
        for head, whole, mixing, scale in zip(heads, wholes, mixings, scales):
            _, x_ref, mix_ref, out_ref = head
            if sweep < ITERS - 1:
                x_ref[...] = advance(whole, mixing, whole, scale)
                continue
            mix_ref[...] = mixing
            rows, cols = out_ref.shape
            own_rows = pl.ds(pl.multiple_of(own_row * rows, rows), rows)
            own_cols = pl.ds(pl.multiple_of(own_col * cols, cols), cols)
            out_ref[...] = advance(
                x_ref[own_rows, own_cols], mix_ref[own_rows, :], x_ref[:, own_cols]
            )


def add_into(target, others, count):
    def step(i, carry):
        total = target[i].astype(jnp.float32)
        for other in others:
            total += other[i].astype(jnp.float32)
        target[i] = total.astype(target.dtype)
        return carry

    lax.fori_loop(0, count, step, 0)


def kernel(
    lat_kv, lat_q, grad_kv, grad_q, mom_kv, mom_q,
    x_k, x_q, new_k, new_q,
    lk, lq, gk, gq, parts, ones, twos, threes, sum_k, sum_q, held_k, held_q,
    in_sem, gk_sem, gq_sem, send_sem, recv_sem, ag_send, ag_recv,
):
    me = lax.axis_index("dp")
    core = lax.axis_index("tensor")
    where = {"x": me // 16, "z": lax.rem(me // 4, 4), "y": lax.rem(me, 4)}
    low = lax.rem(me, 2)
    twin = me + 1 - 2 * low
    group = ((me, 1 - core), (twin, core), (twin, 1 - core))

    barrier = pltpu.get_barrier_semaphore()
    friends = [(shifted(where, a, s), core) for a in "xyz" for s in (1, 2, 3)]
    friends += [group[0], group[2]]
    for friend in friends:
        pl.semaphore_signal(barrier, inc=1, device_id=friend, device_id_type=MESH)

    def fetch(source, target, sems, width, i):
        u = lax.rem(where["x"] + i // 4, 4) * 4 + lax.rem(where["z"] + lax.rem(i, 4), 4)
        at = pl.multiple_of(u * width, 128)
        return pltpu.make_async_copy(source.at[:, pl.ds(at, width)], target.at[i], sems.at[i])

    fetch_q = functools.partial(fetch, grad_q, gq, gq_sem, 4 * Q_ROWS)
    fetch_k = functools.partial(fetch, grad_kv, gk, gk_sem, 4 * KV_ROWS)
    load_lq = [
        pltpu.make_async_copy(
            lat_q.at[:, pl.ds(k * SLAB, SLAB)], lq.at[:, pl.ds(k * SLAB, SLAB)], in_sem.at[k]
        )
        for k in range(3)
    ]
    load_lk = pltpu.make_async_copy(lat_kv, lk, in_sem.at[3])
    load_held = [
        pltpu.make_async_copy(mom_kv, held_k, in_sem.at[4]),
        pltpu.make_async_copy(mom_q, held_q, in_sem.at[5]),
    ]
    load_lq[0].start()
    for i in (8, 9, 10, 11):
        fetch_q(i).start()
    load_lq[2].start()
    for i in (0, 1, 2, 3):
        fetch_q(i).start()
    load_lq[1].start()
    for i in (6, 14, 12, 13, 15, 4, 5, 7):
        fetch_q(i).start()

    started = []

    class Chunk:
        def __init__(self, index, ring):
            self.index, self.ring = index, ring
            self.parts, self.ones = parts[index], ones[index]
            self.twos, self.threes = twos[index], threes[index]
            self.copies, self.split = {}, set()

        def go(self, s, slot, source, target, axis, step):
            copy = pltpu.make_async_remote_copy(
                src_ref=source,
                dst_ref=target,
                send_sem=send_sem.at[self.index, s, slot],
                recv_sem=recv_sem.at[self.index, s, slot],
                device_id=(shifted(where, axis, step), core),
                device_id_type=MESH,
            )
            copy.start()
            started.append(copy)
            self.copies[s, slot] = copy

        def arrived(self, s, *slots):
            for slot in slots:
                self.copies[s, slot].wait_recv()

        def far(self, s, half):
            part, got, axis = self.parts[s], self.ones[s], ORDERS[s][0]
            step = 1 if half == 0 else -1
            self.go(s, half, part.at[2, pl.ds(2 * half, 2)], got.at[half], axis, step)

        def far_one(self, s, b):
            part, got, axis = self.parts[s], self.ones[s], ORDERS[s][0]
            half, at = b // 2, b % 2
            slot = FOURTH + half if at else half
            step = 1 if half == 0 else -1
            self.go(s, slot, part.at[2, b], got.at[half, at], axis, step)
            self.split.add(s)

        def far_in(self, s, half):
            self.arrived(s, half)
            if s in self.split:
                self.arrived(s, FOURTH + half)

        def near(self, s, half):
            part, got, axis = self.parts[s], self.ones[s], ORDERS[s][0]
            if half == 0:
                self.go(s, 3, part.at[3, pl.ds(0, 2)], got.at[3], axis, -1)
            else:
                self.go(s, 2, part.at[1, pl.ds(2, 2)], got.at[2], axis, 1)

        def relay1(self, s):
            part, got, axis = self.parts[s], self.ones[s], ORDERS[s][0]
            self.far_in(s, 0)
            for b in range(2):
                add_into(part.at[1, b], [got.at[0, b]], 4)
            self.go(s, 4, part.at[1, pl.ds(0, 2)], got.at[4], axis, 1)
            self.far_in(s, 1)
            for b in range(2):
                add_into(part.at[3, 2 + b], [got.at[1, b]], 4)
            self.go(s, 5, part.at[3, pl.ds(2, 2)], got.at[5], axis, -1)

        def second(self, s):
            part, got, two, axis = self.parts[s], self.ones[s], self.twos[s], ORDERS[s][1]
            self.arrived(s, 2, 5)
            add_into(part.at[0, 2], [got.at[2, 0], got.at[5, 0]], 4)
            if self.ring:
                for half, step in ((0, 1), (1, -1)):
                    self.go(
                        s, SECOND + half, part.at[0, 2, pl.ds(2 * half, 2)],
                        two.at[pl.ds(2 * half, 2)], axis, step,
                    )
            else:
                self.go(s, SECOND + 1, part.at[0, 2], two.at[pl.ds(4, 4)], axis, 2)
            add_into(part.at[0, 3], [got.at[2, 1], got.at[5, 1]], 4)
            if self.ring:
                self.go(s, SECOND + 3, part.at[0, 3, pl.ds(0, 2)], two.at[pl.ds(6, 2)], axis, -1)
            else:
                self.go(s, SECOND + 2, part.at[0, 3], two.at[pl.ds(8, 4)], axis, 3)
            self.arrived(s, 3, 4)
            add_into(part.at[0, 1], [got.at[3, 1], got.at[4, 1]], 4)
            if self.ring:
                self.go(s, SECOND + 2, part.at[0, 1, pl.ds(2, 2)], two.at[pl.ds(4, 2)], axis, 1)
            else:
                self.go(s, SECOND, part.at[0, 1], two.at[pl.ds(0, 4)], axis, 1)
            add_into(part.at[0, 0], [got.at[3, 0], got.at[4, 0]], 4)

        def relay2(self, s):
            part, two, axis = self.parts[s], self.twos[s], ORDERS[s][1]
            for half, b, step in ((0, 1, 1), (1, 3, -1)):
                held = part.at[0, b, pl.ds(2 * half, 2)]
                self.arrived(s, SECOND + half)
                add_into(held, [two.at[pl.ds(2 * half, 2)]], 2)
                self.go(
                    s, SECOND + 4 + half, held, two.at[pl.ds(8 + 2 * half, 2)], axis, step
                )

        def third(self, s):
            part, two, three, axis = self.parts[s], self.twos[s], self.threes[s], ORDERS[s][2]
            if self.ring:
                for half, slots in ((0, (3, 4)), (1, (2, 5))):
                    self.arrived(s, *(SECOND + k for k in slots))
                    add_into(
                        part.at[0, 0, pl.ds(2 * half, 2)],
                        [two.at[pl.ds(2 * k, 2)] for k in slots], 2,
                    )
            else:
                self.arrived(s, *(SECOND + k for k in range(3)))
                add_into(part.at[0, 0], [two.at[pl.ds(4 * k, 4)] for k in range(3)], 4)
            for c in (2, 1, 3):
                self.go(s, THIRD - 1 + c, part.at[0, 0, c], three.at[c - 1], axis, c)

        def total(self, s):
            part, three = self.parts[s], self.threes[s]
            self.arrived(s, *(THIRD + k for k in range(3)))
            total = part[0, 0, 0].astype(jnp.float32)
            for c in range(3):
                total += three[c].astype(jnp.float32)
            return total

    chunks = {name: Chunk(at, name in RINGS) for at, name in enumerate(("q0", "q1", "k0", "k1"))}

    def store(pair, cuts, stride, s, i, term, lanes_from):
        xr, zr = i // 4, lax.rem(i, 4)
        at, rows = cuts[s]
        for y in range(4):
            place = {"x": xr, "z": zr, "y": lax.rem(y - where["y"] + 4, 4)}
            place = tuple(place[a] for a in ORDERS[s])
            for half in range(2):
                lane = lanes_from + half * LANES
                chunks[pair[half]].parts[s][place] = term[
                    y * stride + at:y * stride + at + rows, lane:lane + LANES
                ]

    def slab_q(s, unit_of, count):
        def step(j, carry):
            i = unit_of(j)
            term = lax.dot_general(
                gq[i], lq[:, s * SLAB:(s + 1) * SLAB], (((0,), (0,)), ((), ())),
                preferred_element_type=jnp.float32,
            ).astype(jnp.bfloat16)
            store(("q0", "q1"), Q_CUT, Q_ROWS, s, i, term, 0)
            return carry

        lax.fori_loop(0, count, step, 0)

    def unit_k(i, carry):
        fetch_k(i).wait()
        term = lax.dot_general(
            gk[i], lk[...], (((0,), (0,)), ((), ())), preferred_element_type=jnp.float32
        ).astype(jnp.bfloat16)
        for s in range(3):
            store(("k0", "k1"), KV_CUT, KV_ROWS, s, i, term, 0)
        return carry

    q_ready = []

    def need_q(*units):
        for i in units:
            if i not in q_ready:
                q_ready.append(i)
                fetch_q(i).wait()

    def each_q(act, *args):
        for name in ("q0", "q1"):
            getattr(chunks[name], act)(*args)

    load_lq[0].wait()
    need_q(8, 9)
    slab_q(0, lambda j: 8 + j, 2)
    pl.semaphore_wait(barrier, len(friends))
    each_q("far", 0, 0)
    need_q(10, 11)
    slab_q(0, lambda j: 10 + j, 2)
    each_q("far", 0, 1)
    load_lq[2].wait()
    slab_q(2, lambda j: 8 + j, 4)
    each_q("far_one", 2, 2)
    need_q(0, 1, 2, 3)
    slab_q(2, lambda j: j, 4)
    each_q("far_one", 2, 0)
    load_lq[1].wait()
    need_q(6, 14)
    slab_q(1, lambda j: 2 + 4 * j, 4)
    each_q("far", 1, 0)
    each_q("far", 1, 1)
    load_lk.start()
    for i in range(16):
        fetch_k(i).start()
    for load in load_held:
        load.start()
    need_q(12, 13, 15)
    slab_q(2, lambda j: 12 + j, 4)
    each_q("far_one", 2, 3)
    need_q(4, 5, 7)
    slab_q(2, lambda j: 4 + j, 4)
    each_q("far_one", 2, 1)
    slab_q(0, lambda j: 4 + j, 4)
    each_q("near", 0, 1)
    slab_q(0, lambda j: 12 + j, 4)
    each_q("near", 0, 0)
    slab_q(1, lambda j: 1 + 4 * j, 4)
    each_q("near", 1, 1)
    slab_q(1, lambda j: 3 + 4 * j, 4)
    each_q("near", 1, 0)
    each_q("near", 2, 1)
    each_q("near", 2, 0)
    slab_q(0, lambda j: j, 4)
    slab_q(1, lambda j: 4 * j, 4)

    sets = {
        "q": (0, sum_q, held_q, new_q, x_q, Q_ROWS, Q_COLS),
        "k": (1, sum_k, held_k, new_k, x_k, KV_ROWS, KV_COLS),
    }

    def slot(kind, owner, c):
        _, _, _, _, x_ref, rows, cols = sets[kind]
        return x_ref.at[
            pl.ds(pl.multiple_of(lax.rem(owner, 2) * rows, rows), rows),
            pl.ds(pl.multiple_of(c * cols, cols), cols),
        ]

    def group_copy(kind, k, source, target):
        return pltpu.make_async_remote_copy(
            src_ref=source,
            dst_ref=target,
            send_sem=ag_send.at[sets[kind][0], k],
            recv_sem=ag_recv.at[sets[kind][0], k],
            device_id=group[k],
            device_id_type=MESH,
        )

    def gather(kind):
        index, total, held, new_ref, _, _, _ = sets[kind]
        load_held[1 - index].wait()
        gradient = total[...]
        renewed = momentum_rate * held[...] + gradient
        prepared = gradient + momentum_rate * renewed
        mine = slot(kind, me, core)
        mine[...] = prepared.astype(jnp.bfloat16)
        for k in (1, 0) if kind == "q" else (1, 2, 0):
            copy = group_copy(kind, k, mine, mine)
            copy.start()
            started.append(copy)
        new_ref[...] = renewed

    def forward(kind):
        theirs = slot(kind, *group[1])
        group_copy(kind, 1, slot(kind, me, core), theirs).wait_recv()
        copy = pltpu.make_async_remote_copy(
            src_ref=theirs,
            dst_ref=theirs,
            send_sem=ag_send.at[sets[kind][0], 2],
            recv_sem=ag_recv.at[sets[kind][0], 2],
            device_id=group[0],
            device_id_type=MESH,
        )
        copy.start()
        started.append(copy)

    def end(kind):
        for k in (0, 2) if kind == "q" else (0, 1, 2):
            group_copy(kind, k, slot(kind, me, core), slot(kind, *group[k])).wait_recv()

    for item in PLAN:
        act, name = item.split()
        if act == "products":
            load_lk.wait()
            lax.fori_loop(0, 16, unit_k, 0)
        elif act in ("far", "near"):
            for s in range(3):
                for half in range(2):
                    getattr(chunks[name], act)(s, half)
        elif act in ("relay1", "second", "relay2", "third"):
            for s in range(3):
                getattr(chunks[name], act)(s)
        elif act == "last":
            half = int(name[1])
            for s in range(3):
                total = chunks[name].total(s)
                if name[0] == "q":
                    lane = s * SLAB + half * LANES
                    sum_q[:, lane:lane + LANES] = total
                else:
                    at, rows = KV_CUT[s]
                    sum_k[at:at + rows, half * LANES:(half + 1) * LANES] = total
        elif act == "gather":
            gather(name)
        elif act == "forward":
            forward(name)
        elif act == "end":
            end(name)
    for copy in started:
        copy.wait_send()


def closing(
    prep_k, prep_q, new_k, new_q, out_uk, out_nk, out_uq, out_nq,
    x_k, x_q, mix_k, mix_q, up_k, up_q, sem,
):
    moves = ((new_k, out_nk), (new_q, out_nq), (up_k, out_uk), (up_q, out_uq))
    moves = [pltpu.make_async_copy(a, b, sem.at[k]) for k, (a, b) in enumerate(moves)]
    moves[0].start()
    moves[1].start()
    newton(((prep_k, x_k, mix_k, up_k), (prep_q, x_q, mix_q, up_q)))
    moves[2].start()
    moves[3].start()
    for move in moves:
        move.wait()


def per_device(latent_kv, latent_q, grad_kv, grad_q, momentum_kv, momentum_q):
    arrays = (latent_kv, latent_q, grad_kv, grad_q, momentum_kv, momentum_q)
    arrays = [pltpu.with_memory_space_constraint(array, pltpu.HBM) for array in arrays]
    low, full = jnp.bfloat16, jnp.float32
    cuts = (Q_CUT, Q_CUT, KV_CUT, KV_CUT)

    def cells(*lead):
        return [[pltpu.VMEM(lead + (rows, LANES), low) for _, rows in cut] for cut in cuts]

    vmem = pl.BlockSpec(memory_space=pltpu.VMEM)
    hbm = pl.BlockSpec(memory_space=pl.ANY)
    middle = pl.pallas_call(
        kernel,
        out_shape=(
            pltpu.VMEM((2 * KV_ROWS, 2 * KV_COLS), low),
            pltpu.VMEM((2 * Q_ROWS, 2 * Q_COLS), low),
            pltpu.VMEM((KV_ROWS, KV_COLS), full),
            pltpu.VMEM((Q_ROWS, Q_COLS), full),
        ),
        in_specs=[hbm] * 6,
        out_specs=(vmem,) * 4,
        scratch_shapes=[
            pltpu.VMEM((TOK, KV_COLS), low),
            pltpu.VMEM((TOK, Q_COLS), low),
            pltpu.VMEM((16, TOK, 4 * KV_ROWS), low),
            pltpu.VMEM((16, TOK, 4 * Q_ROWS), low),
            cells(4, 4, 4),
            cells(6, 2, 4),
            cells(12),
            cells(3),
            pltpu.VMEM((KV_ROWS, KV_COLS), full),
            pltpu.VMEM((Q_ROWS, Q_COLS), full),
            pltpu.VMEM((KV_ROWS, KV_COLS), full),
            pltpu.VMEM((Q_ROWS, Q_COLS), full),
            pltpu.SemaphoreType.DMA((6,)),
            pltpu.SemaphoreType.DMA((16,)),
            pltpu.SemaphoreType.DMA((16,)),
            pltpu.SemaphoreType.DMA((4, 3, SLOTS)),
            pltpu.SemaphoreType.DMA((4, 3, SLOTS)),
            pltpu.SemaphoreType.DMA((2, 3)),
            pltpu.SemaphoreType.DMA((2, 3)),
        ],
        compiler_params=pltpu.CompilerParams(
            collective_id=0, has_side_effects=True, vmem_limit_bytes=50 * 2**20
        ),
        name="sum_all",
    )(*arrays)
    return pl.pallas_call(
        closing,
        out_shape=(
            jax.ShapeDtypeStruct((KV_ROWS, KV_COLS), low),
            jax.ShapeDtypeStruct((KV_ROWS, KV_COLS), full),
            jax.ShapeDtypeStruct((Q_ROWS, Q_COLS), low),
            jax.ShapeDtypeStruct((Q_ROWS, Q_COLS), full),
        ),
        in_specs=[vmem] * 4,
        out_specs=(hbm,) * 4,
        scratch_shapes=[
            pltpu.VMEM((2 * KV_ROWS, 2 * KV_COLS), low),
            pltpu.VMEM((2 * Q_ROWS, 2 * Q_COLS), low),
            pltpu.VMEM((2 * KV_ROWS, 2 * KV_ROWS), low),
            pltpu.VMEM((2 * Q_ROWS, 2 * Q_ROWS), low),
            pltpu.VMEM((KV_ROWS, KV_COLS), low),
            pltpu.VMEM((Q_ROWS, Q_COLS), low),
            pltpu.SemaphoreType.DMA((4,)),
        ],
        compiler_params=pltpu.CompilerParams(vmem_limit_bytes=24 * 2**20),
        name="closing",
    )(*middle)


def solution(mesh):
    in_specs = (
        P("dp", "tensor"),
        P("dp", "tensor"),
        P("dp", None),
        P("dp", None),
        P("dp", "tensor"),
        P("dp", "tensor"),
    )
    out_specs = (P("dp", "tensor"), P("dp", "tensor"), P("dp", "tensor"), P("dp", "tensor"))
    return jax.shard_map(
        per_device, mesh=mesh, in_specs=in_specs, out_specs=out_specs, check_vma=False
    )
```

time: 712 us -> 85.6 us (0.12)
  waiting for transfers between devices: 616 us -> 0 us
  Pallas kernels: 0 us -> 84.8 us
  blocking collectives: 35.1 us -> 0 us
  matrix products: 28.6 us -> 0 us
  between operations: 16.9 us -> 0.64 us
  starting transfers between devices: 9.66 us -> 0 us
    reduce_scatter x2 -> x0, waiting for transfers between devices: 594 us -> none  [the longest x1 311 us: per_device(): lax.psum_scatter(half_terms(grad_kv, latent_kv), 'dp', scatter_dimension=...]
    pallas_call x0 -> x2, Pallas kernels: none -> 84.8 us  [the longest x1 80.1 us: per_device(): pl.pallas_call(kernel, out_shape=(pltpu.VMEM((2 * KV_ROWS, 2 * KV_COLS),...]
    psum x6 -> x0, blocking collectives: 35.1 us -> none  [the longest x5 29.7 us: split_rows(): grams = lax.psum((outer_self(stacked[0]), outer_self(stacked[1])), 'tensor')]
    dot_general x32 -> x0, matrix products: 28.6 us -> none  [the longest x2 21.1 us: half_terms(): lax.dot_general(grads, latents, (((0,), (0,)), ((), ())), preferred_eleme...]
    ppermute x12 -> x0, waiting for transfers between devices: 22.6 us -> none  [from_partner(): lax.ppermute(shard, axis, [(i, i ^ 1 << bit) for i in range(lax.axis_size...]
    ppermute x12 -> x0, starting transfers between devices: 9.58 us -> none  [from_partner(): lax.ppermute(shard, axis, [(i, i ^ 1 << bit) for i in range(lax.axis_size...]
  transfers between devices with their start and end apart: 14 -> 0, of which waited for: 13 -> 0; matrix products, arithmetic and copies ran while one was open for 2% -> 0% of each run, Pallas kernels for 0% -> 0%
where the time goes in v2:
time: 85.6 us; the launch traced here: 85.5 us
  Pallas kernels  84.8 us (99%)
    pallas_call x1, Pallas kernels, per_device(): pl.pallas_call(kernel, out_shape=(pltpu.VMEM((2 * KV_ROWS, 2 * KV_COLS),...  80.1 us
    pallas_call x1, Pallas kernels, per_device(): pl.pallas_call(closing, out_shape=(jax.ShapeDtypeStruct((KV_ROWS, KV_COLS...  4.73 us

profile of v2, /device:TPU:1, one launch (start us, length us, event | category | flops | bytes accessed | tf_op | source)
XLA Modules:
  0.0 85.5 jit_solution(9245800340186140244)
XLA Ops:
  0.6 80.1 %sum_all.1 = (bf16[256,512]{1,0:T(8,128)(2,1)S(1)}, bf16[192,1536]{1,0:T(8,128)(2,1)S(1)}, f32[128,256]{1,0:T(8,128)S(1)}, f32[96,768]{1,0:T(8,128)S(1)}) custom-call(bf16[512,256]{1,0:T(8,128)(2,1)} %lat_kv.1, bf16[512,768]{1,0:T(8,128)(2,1)} %lat_q.1, bf16[512,8192]{1,0:T(8,128)(2,1)} %grad_kv.1, bf16[512,6144]{1,0:T(8,128)(2,1)} %grad_q.1, ...), custom_call_target="tpu_custom_call" | custom-call | tf_op jit(solution)/shard_map/sum_all/pallas_call | solution.py:480
  80.8 4.7 %closing.1 = (bf16[128,256]{1,0:T(8,128)(2,1)}, f32[128,256]{1,0:T(8,128)}, bf16[96,768]{1,0:T(8,128)(2,1)}, f32[96,768]{1,0:T(8,128)}) custom-call(bf16[256,512]{1,0:T(8,128)(2,1)S(1)} %get-tuple-element.8.prep_k, bf16[192,1536]{1,0:T(8,128)(2,1)S(1)} %get-tuple-element.9.prep_q, f32[128,256]{1,0:T(8,128)S(1)} %get-tuple-element.10.new_k, ...), custom_call_target="tpu_custom_call" | custom-call | tf_op jit(solution)/shard_map/closing/pallas_call | solution.py:516

commit v3 on v2

--- a/solution.py
+++ b/solution.py
@@ -27,13 +27,16 @@
 Q_CUT = ((0, 96),) * 3
 SECOND, THIRD, FOURTH = 6, 12, 15
 SLOTS = 17
-RINGS = ("q0", "q1")
+FORWARDED = ("q0", "q1", "k0")
+RINGS = ("q0", "q1", "k0")
 
 PLAN = (
-    "relay1 q0", "products k", "far k0", "far k1", "near k1", "second q0", "relay1 q1",
-    "near k0", "relay1 k0", "relay2 q0", "relay1 k1", "second q1", "third q0", "relay2 q1",
-    "second k0", "third q1", "second k1", "third k0", "last q1", "last q0", "gather q",
-    "third k1", "last k0", "last k1", "gather k", "forward q", "end q", "end k",
+    "near q1", "relay1 q1", "relay1 q0", "products k", "far k0", "near k0", "second q1",
+    "second q0", "relay1 k0", "far k1", "relay2 q0", "relay2 q1", "second k0", "near k1",
+    "relay1 k1", "third q1", "third q0", "relay2 k0", "second k1", "last q0", "gather q0",
+    "third k0", "third k1", "last q1", "gather q1", "last k0", "gather k0", "last k1",
+    "gather k1", "forward q1", "forward q0", "end q0", "forward k0", "end k0", "end k1",
+    "end q1",
 )
 
 
@@ -92,9 +95,13 @@
             rows, cols = out_ref.shape
             own_rows = pl.ds(pl.multiple_of(own_row * rows, rows), rows)
             own_cols = pl.ds(pl.multiple_of(own_col * cols, cols), cols)
-            out_ref[...] = advance(
+            own = advance(
                 x_ref[own_rows, own_cols], mix_ref[own_rows, :], x_ref[:, own_cols]
             )
+            slabs = cols // (2 * LANES)
+            for at in range(2 * slabs):
+                lane = (at % slabs * 2 + at // slabs) * LANES
+                out_ref[:, lane:lane + LANES] = own[:, at * LANES:(at + 1) * LANES]
 
 
 def add_into(target, others, count):
@@ -278,7 +285,7 @@
     chunks = {name: Chunk(at, name in RINGS) for at, name in enumerate(("q0", "q1", "k0", "k1"))}
 
     def store(pair, cuts, stride, s, i, term, lanes_from):
-        xr, zr = i // 4, lax.rem(i, 4)
+        xr, zr = i // 4, i % 4
         at, rows = cuts[s]
         for y in range(4):
             place = {"x": xr, "z": zr, "y": lax.rem(y - where["y"] + 4, 4)}
@@ -290,24 +297,25 @@
                 ]
 
     def slab_q(s, unit_of, count):
-        def step(j, carry):
-            i = unit_of(j)
+        for i in (unit_of(j) for j in range(count)):
             term = lax.dot_general(
                 gq[i], lq[:, s * SLAB:(s + 1) * SLAB], (((0,), (0,)), ((), ())),
                 preferred_element_type=jnp.float32,
             ).astype(jnp.bfloat16)
             store(("q0", "q1"), Q_CUT, Q_ROWS, s, i, term, 0)
-            return carry
-
-        lax.fori_loop(0, count, step, 0)
-
-    def unit_k(i, carry):
-        fetch_k(i).wait()
+
+    def unit_k(i):
         term = lax.dot_general(
             gk[i], lk[...], (((0,), (0,)), ((), ())), preferred_element_type=jnp.float32
         ).astype(jnp.bfloat16)
         for s in range(3):
             store(("k0", "k1"), KV_CUT, KV_ROWS, s, i, term, 0)
+
+    def units_k(j, carry):
+        for i in range(4):
+            fetch_k(4 * j + i).wait()
+        for i in range(4):
+            unit_k(4 * j + i)
         return carry
 
     q_ready = []
@@ -322,14 +330,15 @@
         for name in ("q0", "q1"):
             getattr(chunks[name], act)(*args)
 
+    big, small = chunks["q0"], chunks["q1"]
     load_lq[0].wait()
     need_q(8, 9)
     slab_q(0, lambda j: 8 + j, 2)
     pl.semaphore_wait(barrier, len(friends))
-    each_q("far", 0, 0)
+    big.far(0, 0)
     need_q(10, 11)
     slab_q(0, lambda j: 10 + j, 2)
-    each_q("far", 0, 1)
+    big.far(0, 1)
     load_lq[2].wait()
     slab_q(2, lambda j: 8 + j, 4)
     each_q("far_one", 2, 2)
@@ -339,91 +348,100 @@
     load_lq[1].wait()
     need_q(6, 14)
     slab_q(1, lambda j: 2 + 4 * j, 4)
-    each_q("far", 1, 0)
-    each_q("far", 1, 1)
+    big.far(1, 0)
+    big.far(1, 1)
     load_lk.start()
     for i in range(16):
         fetch_k(i).start()
     for load in load_held:
         load.start()
-    need_q(12, 13, 15)
+    need_q(4, 5, 7, 12, 13, 15)
+    slab_q(0, lambda j: 6 + j, 2)
+    big.near(0, 1)
+    slab_q(0, lambda j: 12 + j, 2)
+    big.near(0, 0)
+    small.far(0, 0)
+    small.far(0, 1)
     slab_q(2, lambda j: 12 + j, 4)
-    each_q("far_one", 2, 3)
-    need_q(4, 5, 7)
+    big.far_one(2, 3)
+    big.near(2, 1)
     slab_q(2, lambda j: 4 + j, 4)
-    each_q("far_one", 2, 1)
-    slab_q(0, lambda j: 4 + j, 4)
-    each_q("near", 0, 1)
-    slab_q(0, lambda j: 12 + j, 4)
-    each_q("near", 0, 0)
+    big.far_one(2, 1)
+    big.near(2, 0)
+    small.far_one(2, 3)
+    small.far_one(2, 1)
     slab_q(1, lambda j: 1 + 4 * j, 4)
-    each_q("near", 1, 1)
+    big.near(1, 1)
     slab_q(1, lambda j: 3 + 4 * j, 4)
-    each_q("near", 1, 0)
-    each_q("near", 2, 1)
-    each_q("near", 2, 0)
+    big.near(1, 0)
+    small.far(1, 0)
+    small.far(1, 1)
+    slab_q(0, lambda j: 4 + j, 2)
+    slab_q(0, lambda j: 14 + j, 2)
     slab_q(0, lambda j: j, 4)
     slab_q(1, lambda j: 4 * j, 4)
 
-    sets = {
-        "q": (0, sum_q, held_q, new_q, x_q, Q_ROWS, Q_COLS),
-        "k": (1, sum_k, held_k, new_k, x_k, KV_ROWS, KV_COLS),
+    kinds = {
+        "q": (sum_q, held_q, new_q, x_q, Q_ROWS, 3 * LANES),
+        "k": (sum_k, held_k, new_k, x_k, KV_ROWS, LANES),
     }
 
-    def slot(kind, owner, c):
-        _, _, _, _, x_ref, rows, cols = sets[kind]
+    def slot(name, owner, c):
+        _, _, _, x_ref, rows, cols = kinds[name[0]]
         return x_ref.at[
             pl.ds(pl.multiple_of(lax.rem(owner, 2) * rows, rows), rows),
-            pl.ds(pl.multiple_of(c * cols, cols), cols),
+            pl.ds(pl.multiple_of((c * 2 + int(name[1])) * cols, LANES), cols),
         ]
 
-    def group_copy(kind, k, source, target):
+    def group_copy(name, k, source, target, way=None):
+        index = chunks[name].index
         return pltpu.make_async_remote_copy(
             src_ref=source,
             dst_ref=target,
-            send_sem=ag_send.at[sets[kind][0], k],
-            recv_sem=ag_recv.at[sets[kind][0], k],
-            device_id=group[k],
+            send_sem=ag_send.at[index, k],
+            recv_sem=ag_recv.at[index, k],
+            device_id=group[k if way is None else way],
             device_id_type=MESH,
         )
 
-    def gather(kind):
-        index, total, held, new_ref, _, _, _ = sets[kind]
-        load_held[1 - index].wait()
-        gradient = total[...]
-        renewed = momentum_rate * held[...] + gradient
-        prepared = gradient + momentum_rate * renewed
-        mine = slot(kind, me, core)
-        mine[...] = prepared.astype(jnp.bfloat16)
-        for k in (1, 0) if kind == "q" else (1, 2, 0):
-            copy = group_copy(kind, k, mine, mine)
+    def gather(name):
+        total, held, new_ref, x_ref, rows, cols = kinds[name[0]]
+        if name in ("q0", "k0"):
+            load_held["kq".index(name[0])].wait()
+        for t in range(cols // LANES):
+            at = pl.ds((2 * t + int(name[1])) * LANES, LANES)
+            gradient = total[:, at]
+            renewed = momentum_rate * held[:, at] + gradient
+            prepared = gradient + momentum_rate * renewed
+            new_ref[:, at] = renewed
+            part = pl.ds(
+                pl.multiple_of((core * 2 + int(name[1])) * cols + t * LANES, LANES), LANES
+            )
+            x_ref[pl.ds(pl.multiple_of(low * rows, rows), rows), part] = prepared.astype(
+                jnp.bfloat16
+            )
+        mine = slot(name, me, core)
+        for k in (1, 0) if name in FORWARDED else (1, 2, 0):
+            copy = group_copy(name, k, mine, mine)
             copy.start()
             started.append(copy)
-        new_ref[...] = renewed
-
-    def forward(kind):
-        theirs = slot(kind, *group[1])
-        group_copy(kind, 1, slot(kind, me, core), theirs).wait_recv()
-        copy = pltpu.make_async_remote_copy(
-            src_ref=theirs,
-            dst_ref=theirs,
-            send_sem=ag_send.at[sets[kind][0], 2],
-            recv_sem=ag_recv.at[sets[kind][0], 2],
-            device_id=group[0],
-            device_id_type=MESH,
-        )
+
+    def forward(name):
+        theirs = slot(name, *group[1])
+        group_copy(name, 1, slot(name, me, core), theirs).wait_recv()
+        copy = group_copy(name, 2, theirs, theirs, 0)
         copy.start()
         started.append(copy)
 
-    def end(kind):
-        for k in (0, 2) if kind == "q" else (0, 1, 2):
-            group_copy(kind, k, slot(kind, me, core), slot(kind, *group[k])).wait_recv()
+    def end(name):
+        for k in (0, 2) if name in FORWARDED else (0, 1, 2):
+            group_copy(name, k, slot(name, me, core), slot(name, *group[k])).wait_recv()
 
     for item in PLAN:
         act, name = item.split()
         if act == "products":
             load_lk.wait()
-            lax.fori_loop(0, 16, unit_k, 0)
+            lax.fori_loop(0, 4, units_k, 0)
         elif act in ("far", "near"):
             for s in range(3):
                 for half in range(2):
@@ -505,8 +523,8 @@
             pltpu.SemaphoreType.DMA((16,)),
             pltpu.SemaphoreType.DMA((4, 3, SLOTS)),
             pltpu.SemaphoreType.DMA((4, 3, SLOTS)),
-            pltpu.SemaphoreType.DMA((2, 3)),
-            pltpu.SemaphoreType.DMA((2, 3)),
+            pltpu.SemaphoreType.DMA((4, 3)),
+            pltpu.SemaphoreType.DMA((4, 3)),
         ],
         compiler_params=pltpu.CompilerParams(
             collective_id=0, has_side_effects=True, vmem_limit_bytes=50 * 2**20

time: 85.6 us -> 80.7 us (0.943)
  Pallas kernels: 84.8 us -> 79.7 us
    pallas_call x1, Pallas kernels: 80.1 us -> 75 us  [per_device(): pl.pallas_call(kernel, out_shape=(pltpu.VMEM((2 * KV_ROWS, 2 * KV_COLS),...]
where the time goes in v3:
time: 80.7 us; the launch traced here: 80.5 us
  Pallas kernels  79.7 us (99%)
    pallas_call x1, Pallas kernels, per_device(): pl.pallas_call(kernel, out_shape=(pltpu.VMEM((2 * KV_ROWS, 2 * KV_COLS),...  75 us
    pallas_call x1, Pallas kernels, per_device(): pl.pallas_call(closing, out_shape=(jax.ShapeDtypeStruct((KV_ROWS, KV_COLS...  4.73 us

profile of v3, /device:TPU:1, one launch (start us, length us, event | category | flops | bytes accessed | tf_op | source)
XLA Modules:
  0.0 80.5 jit_solution(5920187973995654388)
XLA Ops:
  0.6 75.0 %sum_all.1 = (bf16[256,512]{1,0:T(8,128)(2,1)S(1)}, bf16[192,1536]{1,0:T(8,128)(2,1)S(1)}, f32[128,256]{1,0:T(8,128)S(1)}, f32[96,768]{1,0:T(8,128)S(1)}) custom-call(bf16[512,256]{1,0:T(8,128)(2,1)} %lat_kv.1, bf16[512,768]{1,0:T(8,128)(2,1)} %lat_q.1, bf16[512,8192]{1,0:T(8,128)(2,1)} %grad_kv.1, bf16[512,6144]{1,0:T(8,128)(2,1)} %grad_q.1, ...), custom_call_target="tpu_custom_call" | custom-call | tf_op jit(solution)/shard_map/sum_all/pallas_call | solution.py:498
  75.6 4.7 %closing.1 = (bf16[128,256]{1,0:T(8,128)(2,1)}, f32[128,256]{1,0:T(8,128)}, bf16[96,768]{1,0:T(8,128)(2,1)}, f32[96,768]{1,0:T(8,128)}) custom-call(bf16[256,512]{1,0:T(8,128)(2,1)S(1)} %get-tuple-element.8.prep_k, bf16[192,1536]{1,0:T(8,128)(2,1)S(1)} %get-tuple-element.9.prep_q, f32[128,256]{1,0:T(8,128)S(1)} %get-tuple-element.10.new_k, ...), custom_call_target="tpu_custom_call" | custom-call | tf_op jit(solution)/shard_map/closing/pallas_call | solution.py:534

commit v4 on v3

--- a/solution.py
+++ b/solution.py
@@ -25,8 +25,6 @@
 ORDERS = ("xzy", "zyx", "yxz")
 KV_CUT = ((0, 48), (48, 48), (96, 32))
 Q_CUT = ((0, 96),) * 3
-SECOND, THIRD, FOURTH = 6, 12, 15
-SLOTS = 17
 FORWARDED = ("q0", "q1", "k0")
 RINGS = ("q0", "q1", "k0")
 
@@ -134,13 +132,25 @@
     for friend in friends:
         pl.semaphore_signal(barrier, inc=1, device_id=friend, device_id_type=MESH)
 
-    def fetch(source, target, sems, width, i):
+    def fetch(source, target, sem, width, i):
         u = lax.rem(where["x"] + i // 4, 4) * 4 + lax.rem(where["z"] + lax.rem(i, 4), 4)
         at = pl.multiple_of(u * width, 128)
-        return pltpu.make_async_copy(source.at[:, pl.ds(at, width)], target.at[i], sems.at[i])
-
-    fetch_q = functools.partial(fetch, grad_q, gq, gq_sem, 4 * Q_ROWS)
-    fetch_k = functools.partial(fetch, grad_kv, gk, gk_sem, 4 * KV_ROWS)
+        return pltpu.make_async_copy(source.at[:, pl.ds(at, width)], target.at[i], sem)
+
+    q_sets = ((8, 9), (10, 11), (0, 1, 2, 3), (6, 14), (4, 5, 7, 12, 13, 15))
+
+    def start_q(k):
+        for i in q_sets[k]:
+            fetch(grad_q, gq, gq_sem.at[k], 4 * Q_ROWS, i).start()
+
+    def need_q(k):
+        many = gq.at[pl.ds(0, len(q_sets[k]))]
+        pltpu.make_async_copy(many, many, gq_sem.at[k]).wait()
+
+    def start_k():
+        for i in range(16):
+            fetch(grad_kv, gk, gk_sem.at[i // 4], 4 * KV_ROWS, i).start()
+
     load_lq = [
         pltpu.make_async_copy(
             lat_q.at[:, pl.ds(k * SLAB, SLAB)], lq.at[:, pl.ds(k * SLAB, SLAB)], in_sem.at[k]
@@ -153,131 +163,118 @@
         pltpu.make_async_copy(mom_q, held_q, in_sem.at[5]),
     ]
     load_lq[0].start()
-    for i in (8, 9, 10, 11):
-        fetch_q(i).start()
+    start_q(0)
+    start_q(1)
     load_lq[2].start()
-    for i in (0, 1, 2, 3):
-        fetch_q(i).start()
+    start_q(2)
     load_lq[1].start()
-    for i in (6, 14, 12, 13, 15, 4, 5, 7):
-        fetch_q(i).start()
-
-    started = []
+    start_q(3)
+    start_q(4)
+
+    def take(ref, sem):
+        pltpu.make_async_remote_copy(
+            src_ref=ref, dst_ref=ref, send_sem=sem, recv_sem=sem,
+            device_id=group[0], device_id_type=MESH,
+        ).wait_recv()
+
+    def run(ref, start, count):
+        return ref.at[pl.ds(start, count)]
 
     class Chunk:
         def __init__(self, index, ring):
             self.index, self.ring = index, ring
             self.parts, self.ones = parts[index], ones[index]
             self.twos, self.threes = twos[index], threes[index]
-            self.copies, self.split = {}, set()
-
-        def go(self, s, slot, source, target, axis, step):
-            copy = pltpu.make_async_remote_copy(
+
+        def sem(self, s, stage):
+            return recv_sem.at[self.index, 4 * s + stage]
+
+        def go(self, s, stage, source, target, axis, step):
+            pltpu.make_async_remote_copy(
                 src_ref=source,
                 dst_ref=target,
-                send_sem=send_sem.at[self.index, s, slot],
-                recv_sem=recv_sem.at[self.index, s, slot],
+                send_sem=send_sem.at[self.index, s],
+                recv_sem=self.sem(s, stage) if stage < 4 else recv_sem.at[self.index, 12],
                 device_id=(shifted(where, axis, step), core),
                 device_id_type=MESH,
-            )
-            copy.start()
-            started.append(copy)
-            self.copies[s, slot] = copy
-
-        def arrived(self, s, *slots):
-            for slot in slots:
-                self.copies[s, slot].wait_recv()
+            ).start()
+
+        def sent(self):
+            for s in range(3):
+                take(run(self.parts[s], 0, 63), send_sem.at[self.index, s])
 
         def far(self, s, half):
             part, got, axis = self.parts[s], self.ones[s], ORDERS[s][0]
             step = 1 if half == 0 else -1
-            self.go(s, half, part.at[2, pl.ds(2 * half, 2)], got.at[half], axis, step)
+            self.go(s, 0, run(part, 32 + 8 * half, 8), run(got, 8 * half, 8), axis, step)
 
         def far_one(self, s, b):
             part, got, axis = self.parts[s], self.ones[s], ORDERS[s][0]
-            half, at = b // 2, b % 2
-            slot = FOURTH + half if at else half
-            step = 1 if half == 0 else -1
-            self.go(s, slot, part.at[2, b], got.at[half, at], axis, step)
-            self.split.add(s)
-
-        def far_in(self, s, half):
-            self.arrived(s, half)
-            if s in self.split:
-                self.arrived(s, FOURTH + half)
+            step = 1 if b < 2 else -1
+            self.go(s, 0, run(part, 32 + 4 * b, 4), run(got, 4 * b, 4), axis, step)
 
         def near(self, s, half):
             part, got, axis = self.parts[s], self.ones[s], ORDERS[s][0]
             if half == 0:
-                self.go(s, 3, part.at[3, pl.ds(0, 2)], got.at[3], axis, -1)
+                self.go(s, 1, run(part, 48, 8), run(got, 24, 8), axis, -1)
             else:
-                self.go(s, 2, part.at[1, pl.ds(2, 2)], got.at[2], axis, 1)
+                self.go(s, 1, run(part, 24, 8), run(got, 16, 8), axis, 1)
 
         def relay1(self, s):
             part, got, axis = self.parts[s], self.ones[s], ORDERS[s][0]
-            self.far_in(s, 0)
-            for b in range(2):
-                add_into(part.at[1, b], [got.at[0, b]], 4)
-            self.go(s, 4, part.at[1, pl.ds(0, 2)], got.at[4], axis, 1)
-            self.far_in(s, 1)
-            for b in range(2):
-                add_into(part.at[3, 2 + b], [got.at[1, b]], 4)
-            self.go(s, 5, part.at[3, pl.ds(2, 2)], got.at[5], axis, -1)
+            take(run(got, 0, 16), self.sem(s, 0))
+            add_into(run(part, 16, 8), [run(got, 0, 8)], 8)
+            self.go(s, 1, run(part, 16, 8), run(got, 32, 8), axis, 1)
+            add_into(run(part, 56, 8), [run(got, 8, 8)], 8)
+            self.go(s, 1, run(part, 56, 8), run(got, 40, 8), axis, -1)
 
         def second(self, s):
             part, got, two, axis = self.parts[s], self.ones[s], self.twos[s], ORDERS[s][1]
-            self.arrived(s, 2, 5)
-            add_into(part.at[0, 2], [got.at[2, 0], got.at[5, 0]], 4)
+            take(run(got, 16, 32), self.sem(s, 1))
+            add_into(run(part, 8, 4), [run(got, 16, 4), run(got, 40, 4)], 4)
             if self.ring:
-                for half, step in ((0, 1), (1, -1)):
-                    self.go(
-                        s, SECOND + half, part.at[0, 2, pl.ds(2 * half, 2)],
-                        two.at[pl.ds(2 * half, 2)], axis, step,
-                    )
+                self.go(s, 2, run(part, 8, 2), run(two, 0, 2), axis, 1)
+                self.go(s, 2, run(part, 10, 2), run(two, 2, 2), axis, -1)
             else:
-                self.go(s, SECOND + 1, part.at[0, 2], two.at[pl.ds(4, 4)], axis, 2)
-            add_into(part.at[0, 3], [got.at[2, 1], got.at[5, 1]], 4)
+                self.go(s, 2, run(part, 8, 4), run(two, 4, 4), axis, 2)
+            add_into(run(part, 12, 4), [run(got, 20, 4), run(got, 44, 4)], 4)
             if self.ring:
-                self.go(s, SECOND + 3, part.at[0, 3, pl.ds(0, 2)], two.at[pl.ds(6, 2)], axis, -1)
+                self.go(s, 3, run(part, 12, 2), run(two, 6, 2), axis, -1)
             else:
-                self.go(s, SECOND + 2, part.at[0, 3], two.at[pl.ds(8, 4)], axis, 3)
-            self.arrived(s, 3, 4)
-            add_into(part.at[0, 1], [got.at[3, 1], got.at[4, 1]], 4)
+                self.go(s, 2, run(part, 12, 4), run(two, 8, 4), axis, 3)
+            add_into(run(part, 4, 4), [run(got, 28, 4), run(got, 36, 4)], 4)
             if self.ring:
-                self.go(s, SECOND + 2, part.at[0, 1, pl.ds(2, 2)], two.at[pl.ds(4, 2)], axis, 1)
+                self.go(s, 3, run(part, 6, 2), run(two, 4, 2), axis, 1)
             else:
-                self.go(s, SECOND, part.at[0, 1], two.at[pl.ds(0, 4)], axis, 1)
-            add_into(part.at[0, 0], [got.at[3, 0], got.at[4, 0]], 4)
+                self.go(s, 2, run(part, 4, 4), run(two, 0, 4), axis, 1)
+            add_into(run(part, 0, 4), [run(got, 24, 4), run(got, 32, 4)], 4)
 
         def relay2(self, s):
             part, two, axis = self.parts[s], self.twos[s], ORDERS[s][1]
-            for half, b, step in ((0, 1, 1), (1, 3, -1)):
-                held = part.at[0, b, pl.ds(2 * half, 2)]
-                self.arrived(s, SECOND + half)
-                add_into(held, [two.at[pl.ds(2 * half, 2)]], 2)
-                self.go(
-                    s, SECOND + 4 + half, held, two.at[pl.ds(8 + 2 * half, 2)], axis, step
-                )
+            take(run(two, 0, 4), self.sem(s, 2))
+            add_into(run(part, 4, 2), [run(two, 0, 2)], 2)
+            self.go(s, 3, run(part, 4, 2), run(two, 8, 2), axis, 1)
+            add_into(run(part, 14, 2), [run(two, 2, 2)], 2)
+            self.go(s, 3, run(part, 14, 2), run(two, 10, 2), axis, -1)
 
         def third(self, s):
             part, two, three, axis = self.parts[s], self.twos[s], self.threes[s], ORDERS[s][2]
             if self.ring:
-                for half, slots in ((0, (3, 4)), (1, (2, 5))):
-                    self.arrived(s, *(SECOND + k for k in slots))
-                    add_into(
-                        part.at[0, 0, pl.ds(2 * half, 2)],
-                        [two.at[pl.ds(2 * k, 2)] for k in slots], 2,
-                    )
+                take(run(two, 4, 8), self.sem(s, 3))
+                add_into(run(part, 0, 2), [run(two, 6, 2), run(two, 8, 2)], 2)
+                add_into(run(part, 2, 2), [run(two, 4, 2), run(two, 10, 2)], 2)
             else:
-                self.arrived(s, *(SECOND + k for k in range(3)))
-                add_into(part.at[0, 0], [two.at[pl.ds(4 * k, 4)] for k in range(3)], 4)
+                take(run(two, 0, 12), self.sem(s, 2))
+                add_into(run(part, 0, 4), [run(two, 4 * k, 4) for k in range(3)], 4)
             for c in (2, 1, 3):
-                self.go(s, THIRD - 1 + c, part.at[0, 0, c], three.at[c - 1], axis, c)
+                self.go(s, 4, run(part, c, 1), run(three, c - 1, 1), axis, c)
+
+        def third_in(self):
+            take(run(self.parts[0], 0, 9 if self.index < 2 else 8), recv_sem.at[self.index, 12])
 
         def total(self, s):
             part, three = self.parts[s], self.threes[s]
-            self.arrived(s, *(THIRD + k for k in range(3)))
-            total = part[0, 0, 0].astype(jnp.float32)
+            total = part[0].astype(jnp.float32)
             for c in range(3):
                 total += three[c].astype(jnp.float32)
             return total
@@ -289,7 +286,7 @@
         at, rows = cuts[s]
         for y in range(4):
             place = {"x": xr, "z": zr, "y": lax.rem(y - where["y"] + 4, 4)}
-            place = tuple(place[a] for a in ORDERS[s])
+            place = sum(place[a] * w for a, w in zip(ORDERS[s], (16, 4, 1)))
             for half in range(2):
                 lane = lanes_from + half * LANES
                 chunks[pair[half]].parts[s][place] = term[
@@ -312,50 +309,41 @@
             store(("k0", "k1"), KV_CUT, KV_ROWS, s, i, term, 0)
 
     def units_k(j, carry):
-        for i in range(4):
-            fetch_k(4 * j + i).wait()
+        many = gk.at[pl.ds(0, 4)]
+        pltpu.make_async_copy(many, many, gk_sem.at[j]).wait()
         for i in range(4):
             unit_k(4 * j + i)
         return carry
 
-    q_ready = []
-
-    def need_q(*units):
-        for i in units:
-            if i not in q_ready:
-                q_ready.append(i)
-                fetch_q(i).wait()
-
     def each_q(act, *args):
         for name in ("q0", "q1"):
             getattr(chunks[name], act)(*args)
 
     big, small = chunks["q0"], chunks["q1"]
     load_lq[0].wait()
-    need_q(8, 9)
+    need_q(0)
     slab_q(0, lambda j: 8 + j, 2)
     pl.semaphore_wait(barrier, len(friends))
     big.far(0, 0)
-    need_q(10, 11)
+    need_q(1)
     slab_q(0, lambda j: 10 + j, 2)
     big.far(0, 1)
     load_lq[2].wait()
     slab_q(2, lambda j: 8 + j, 4)
     each_q("far_one", 2, 2)
-    need_q(0, 1, 2, 3)
+    need_q(2)
     slab_q(2, lambda j: j, 4)
     each_q("far_one", 2, 0)
     load_lq[1].wait()
-    need_q(6, 14)
+    need_q(3)
     slab_q(1, lambda j: 2 + 4 * j, 4)
     big.far(1, 0)
     big.far(1, 1)
     load_lk.start()
-    for i in range(16):
-        fetch_k(i).start()
+    start_k()
     for load in load_held:
         load.start()
-    need_q(4, 5, 7, 12, 13, 15)
+    need_q(4)
     slab_q(0, lambda j: 6 + j, 2)
     big.near(0, 1)
     slab_q(0, lambda j: 12 + j, 2)
@@ -393,16 +381,20 @@
             pl.ds(pl.multiple_of((c * 2 + int(name[1])) * cols, LANES), cols),
         ]
 
-    def group_copy(name, k, source, target, way=None):
+    def group_copy(name, k, block, way=None):
         index = chunks[name].index
         return pltpu.make_async_remote_copy(
-            src_ref=source,
-            dst_ref=target,
-            send_sem=ag_send.at[index, k],
-            recv_sem=ag_recv.at[index, k],
+            src_ref=block,
+            dst_ref=block,
+            send_sem=ag_send.at[index],
+            recv_sem=ag_recv.at[index, 1 if k == 1 else 0],
             device_id=group[k if way is None else way],
             device_id_type=MESH,
         )
+
+    def blocks(name, count):
+        _, _, _, x_ref, rows, cols = kinds[name[0]]
+        return x_ref.at[pl.ds(0, rows), pl.ds(0, count * cols)]
 
     def gather(name):
         total, held, new_ref, x_ref, rows, cols = kinds[name[0]]
@@ -422,20 +414,17 @@
             )
         mine = slot(name, me, core)
         for k in (1, 0) if name in FORWARDED else (1, 2, 0):
-            copy = group_copy(name, k, mine, mine)
-            copy.start()
-            started.append(copy)
+            group_copy(name, k, mine).start()
 
     def forward(name):
-        theirs = slot(name, *group[1])
-        group_copy(name, 1, slot(name, me, core), theirs).wait_recv()
-        copy = group_copy(name, 2, theirs, theirs, 0)
-        copy.start()
-        started.append(copy)
+        take(blocks(name, 1), ag_recv.at[chunks[name].index, 1])
+        group_copy(name, 2, slot(name, *group[1]), 0).start()
 
     def end(name):
-        for k in (0, 2) if name in FORWARDED else (0, 1, 2):
-            group_copy(name, k, slot(name, me, core), slot(name, *group[k])).wait_recv()
+        if name not in FORWARDED:
+            take(blocks(name, 1), ag_recv.at[chunks[name].index, 1])
+        take(blocks(name, 2), ag_recv.at[chunks[name].index, 0])
+        take(blocks(name, 3), ag_send.at[chunks[name].index])
 
     for item in PLAN:
         act, name = item.split()
@@ -451,6 +440,7 @@
                 getattr(chunks[name], act)(s)
         elif act == "last":
             half = int(name[1])
+            chunks[name].third_in()
             for s in range(3):
                 total = chunks[name].total(s)
                 if name[0] == "q":
@@ -465,8 +455,8 @@
             forward(name)
         elif act == "end":
             end(name)
-    for copy in started:
-        copy.wait_send()
+    for chunk in chunks.values():
+        chunk.sent()
 
 
 def closing(
@@ -510,8 +500,8 @@
             pltpu.VMEM((TOK, Q_COLS), low),
             pltpu.VMEM((16, TOK, 4 * KV_ROWS), low),
             pltpu.VMEM((16, TOK, 4 * Q_ROWS), low),
-            cells(4, 4, 4),
-            cells(6, 2, 4),
+            cells(64),
+            cells(48),
             cells(12),
             cells(3),
             pltpu.VMEM((KV_ROWS, KV_COLS), full),
@@ -519,12 +509,12 @@
             pltpu.VMEM((KV_ROWS, KV_COLS), full),
             pltpu.VMEM((Q_ROWS, Q_COLS), full),
             pltpu.SemaphoreType.DMA((6,)),
-            pltpu.SemaphoreType.DMA((16,)),
-            pltpu.SemaphoreType.DMA((16,)),
-            pltpu.SemaphoreType.DMA((4, 3, SLOTS)),
-            pltpu.SemaphoreType.DMA((4, 3, SLOTS)),
+            pltpu.SemaphoreType.DMA((4,)),
+            pltpu.SemaphoreType.DMA((5,)),
             pltpu.SemaphoreType.DMA((4, 3)),
-            pltpu.SemaphoreType.DMA((4, 3)),
+            pltpu.SemaphoreType.DMA((4, 13)),
+            pltpu.SemaphoreType.DMA((4,)),
+            pltpu.SemaphoreType.DMA((4, 2)),
         ],
         compiler_params=pltpu.CompilerParams(
             collective_id=0, has_side_effects=True, vmem_limit_bytes=50 * 2**20

time: 80.7 us -> 77.5 us (0.960)
  Pallas kernels: 79.7 us -> 76.5 us
    pallas_call x1, Pallas kernels: 75 us -> 71.8 us  [per_device(): pl.pallas_call(kernel, out_shape=(pltpu.VMEM((2 * KV_ROWS, 2 * KV_COLS),...]
where the time goes in v4:
time: 77.5 us; the launch traced here: 77.3 us
  Pallas kernels  76.5 us (99%)
  between operations  0.8 us (1%)
    pallas_call x1, Pallas kernels, per_device(): pl.pallas_call(kernel, out_shape=(pltpu.VMEM((2 * KV_ROWS, 2 * KV_COLS),...  71.8 us
    pallas_call x1, Pallas kernels, per_device(): pl.pallas_call(closing, out_shape=(jax.ShapeDtypeStruct((KV_ROWS, KV_COLS...  4.73 us

profile of v4, /device:TPU:1, one launch (start us, length us, event | category | flops | bytes accessed | tf_op | source)
XLA Modules:
  0.0 77.3 jit_solution(3039975100458426578)
XLA Ops:
  0.6 71.8 %sum_all.1 = (bf16[256,512]{1,0:T(8,128)(2,1)S(1)}, bf16[192,1536]{1,0:T(8,128)(2,1)S(1)}, f32[128,256]{1,0:T(8,128)S(1)}, f32[96,768]{1,0:T(8,128)S(1)}) custom-call(bf16[512,256]{1,0:T(8,128)(2,1)} %lat_kv.1, bf16[512,768]{1,0:T(8,128)(2,1)} %lat_q.1, bf16[512,8192]{1,0:T(8,128)(2,1)} %grad_kv.1, bf16[512,6144]{1,0:T(8,128)(2,1)} %grad_q.1, ...), custom_call_target="tpu_custom_call" | custom-call | tf_op jit(solution)/shard_map/sum_all/pallas_call | solution.py:488
  72.5 4.7 %closing.1 = (bf16[128,256]{1,0:T(8,128)(2,1)}, f32[128,256]{1,0:T(8,128)}, bf16[96,768]{1,0:T(8,128)(2,1)}, f32[96,768]{1,0:T(8,128)}) custom-call(bf16[256,512]{1,0:T(8,128)(2,1)S(1)} %get-tuple-element.8.prep_k, bf16[192,1536]{1,0:T(8,128)(2,1)S(1)} %get-tuple-element.9.prep_q, f32[128,256]{1,0:T(8,128)S(1)} %get-tuple-element.10.new_k, ...), custom_call_target="tpu_custom_call" | custom-call | tf_op jit(solution)/shard_map/closing/pallas_call | solution.py:524

commit v5 on v4

--- a/solution.py
+++ b/solution.py
@@ -28,13 +28,25 @@
 FORWARDED = ("q0", "q1", "k0")
 RINGS = ("q0", "q1", "k0")
 
+Q0, Q1, K0, K1 = "q0", "q1", "k0", "k1"
+PRODUCTS, OWN, FAR, NEAR, LAST, GATHER, FORWARD, END = range(8)
+RELAY1, SECOND, RELAY2, THIRD = "relay1", "second", "relay2", "third"
 PLAN = (
-    "near q1", "relay1 q1", "relay1 q0", "products k", "far k0", "near k0", "second q1",
-    "second q0", "relay1 k0", "far k1", "relay2 q0", "relay2 q1", "second k0", "near k1",
-    "relay1 k1", "third q1", "third q0", "relay2 k0", "second k1", "last q0", "gather q0",
-    "third k0", "third k1", "last q1", "gather q1", "last k0", "gather k0", "last k1",
-    "gather k1", "forward q1", "forward q0", "end q0", "forward k0", "end k0", "end k1",
-    "end q1",
+    (PRODUCTS, 3), (PRODUCTS, 1), (PRODUCTS, 2), (OWN, 1), (OWN, 0), (RELAY1, Q0, 1),
+    (PRODUCTS, 0), (FAR, K0, 2), (FAR, K1, 0), (FAR, K1, 2), (FAR, K0, 0), (RELAY1, Q0, 0),
+    (RELAY1, Q0, 2), (NEAR, K1, 0), (RELAY1, K1, 0), (NEAR, Q1, 1), (NEAR, Q1, 2),
+    (RELAY1, Q1, 2), (NEAR, Q1, 0), (RELAY1, Q1, 0), (FAR, K0, 1), (NEAR, K0, 2), (RELAY1, K0, 2),
+    (SECOND, Q0, 0), (RELAY1, Q1, 1), (SECOND, Q0, 2), (NEAR, K1, 2), (RELAY1, K1, 2),
+    (SECOND, Q0, 1), (FAR, K1, 1), (NEAR, K0, 0), (RELAY1, K0, 0), (NEAR, K0, 1), (RELAY1, K0, 1),
+    (SECOND, Q1, 2), (SECOND, Q1, 0), (SECOND, Q1, 1), (NEAR, K1, 1), (RELAY1, K1, 1),
+    (RELAY2, Q0, 2), (RELAY2, Q0, 0), (SECOND, K0, 1), (RELAY2, Q1, 0), (RELAY2, Q1, 1),
+    (SECOND, K0, 2), (RELAY2, Q0, 1), (RELAY2, Q1, 2), (RELAY2, K0, 1), (SECOND, K0, 0),
+    (SECOND, K1, 2), (SECOND, K1, 0), (RELAY2, K0, 2), (SECOND, K1, 1), (THIRD, Q0, 2),
+    (THIRD, Q1, 1), (THIRD, Q0, 0), (THIRD, Q0, 1), (RELAY2, K0, 0), (THIRD, Q1, 2),
+    (THIRD, Q1, 0), (THIRD, K0, 1), (THIRD, K1, 1), (THIRD, K1, 0), (THIRD, K1, 2),
+    (THIRD, K0, 0), (LAST, Q0), (GATHER, Q0), (LAST, Q1), (GATHER, Q1), (THIRD, K0, 2),
+    (LAST, K0), (GATHER, K0), (LAST, K1), (GATHER, K1), (FORWARD, Q0), (END, Q0), (FORWARD, Q1),
+    (END, Q1), (FORWARD, K0), (END, K0), (END, K1),
 )
 
 
@@ -171,6 +183,8 @@
     start_q(3)
     start_q(4)
 
+    ways = {(a, k): shifted(where, a, k) for a in "xyz" for k in (1, -1, 2, 3)}
+
     def take(ref, sem):
         pltpu.make_async_remote_copy(
             src_ref=ref, dst_ref=ref, send_sem=sem, recv_sem=sem,
@@ -195,7 +209,7 @@
                 dst_ref=target,
                 send_sem=send_sem.at[self.index, s],
                 recv_sem=self.sem(s, stage) if stage < 4 else recv_sem.at[self.index, 12],
-                device_id=(shifted(where, axis, step), core),
+                device_id=(ways[axis, step], core),
                 device_id_type=MESH,
             ).start()
 
@@ -308,12 +322,11 @@
         for s in range(3):
             store(("k0", "k1"), KV_CUT, KV_ROWS, s, i, term, 0)
 
-    def units_k(j, carry):
+    def units_k(j):
         many = gk.at[pl.ds(0, 4)]
         pltpu.make_async_copy(many, many, gk_sem.at[j]).wait()
         for i in range(4):
             unit_k(4 * j + i)
-        return carry
 
     def each_q(act, *args):
         for name in ("q0", "q1"):
@@ -366,8 +379,6 @@
     small.far(1, 1)
     slab_q(0, lambda j: 4 + j, 2)
     slab_q(0, lambda j: 14 + j, 2)
-    slab_q(0, lambda j: j, 4)
-    slab_q(1, lambda j: 4 * j, 4)
 
     kinds = {
         "q": (sum_q, held_q, new_q, x_q, Q_ROWS, 3 * LANES),
@@ -426,19 +437,22 @@
         take(blocks(name, 2), ag_recv.at[chunks[name].index, 0])
         take(blocks(name, 3), ag_send.at[chunks[name].index])
 
-    for item in PLAN:
-        act, name = item.split()
-        if act == "products":
-            load_lk.wait()
-            lax.fori_loop(0, 4, units_k, 0)
-        elif act in ("far", "near"):
-            for s in range(3):
+    first_products = next(at for act, at, *_ in PLAN if act == PRODUCTS)
+    for act, name, *at in PLAN:
+        if act == PRODUCTS:
+            if name == first_products:
+                load_lk.wait()
+            units_k(name)
+        elif act == OWN:
+            slab_q(name, (lambda j: j, lambda j: 4 * j)[name], 4)
+        elif act in (FAR, NEAR):
+            for s in at:
                 for half in range(2):
-                    getattr(chunks[name], act)(s, half)
-        elif act in ("relay1", "second", "relay2", "third"):
-            for s in range(3):
+                    (chunks[name].far if act == FAR else chunks[name].near)(s, half)
+        elif act in (RELAY1, SECOND, RELAY2, THIRD):
+            for s in at:
                 getattr(chunks[name], act)(s)
-        elif act == "last":
+        elif act == LAST:
             half = int(name[1])
             chunks[name].third_in()
             for s in range(3):
@@ -449,11 +463,11 @@
                 else:
                     at, rows = KV_CUT[s]
                     sum_k[at:at + rows, half * LANES:(half + 1) * LANES] = total
-        elif act == "gather":
+        elif act == GATHER:
             gather(name)
-        elif act == "forward":
+        elif act == FORWARD:
             forward(name)
-        elif act == "end":
+        elif act == END:
             end(name)
     for chunk in chunks.values():
         chunk.sent()

time: 77.5 us -> 76.4 us (0.986)
  Pallas kernels: 76.5 us -> 75.5 us
    pallas_call x1, Pallas kernels: 71.8 us -> 70.8 us  [per_device(): pl.pallas_call(kernel, out_shape=(pltpu.VMEM((2 * KV_ROWS, 2 * KV_COLS),...]
where the time goes in v5:
time: 76.4 us; the launch traced here: 76.3 us
  Pallas kernels  75.5 us (99%)
  between operations  0.8 us (1%)
    pallas_call x1, Pallas kernels, per_device(): pl.pallas_call(kernel, out_shape=(pltpu.VMEM((2 * KV_ROWS, 2 * KV_COLS),...  70.8 us
    pallas_call x1, Pallas kernels, per_device(): pl.pallas_call(closing, out_shape=(jax.ShapeDtypeStruct((KV_ROWS, KV_COLS...  4.73 us

profile of v5, /device:TPU:1, one launch (start us, length us, event | category | flops | bytes accessed | tf_op | source)
XLA Modules:
  0.0 76.3 jit_solution(9141677636685451421)
XLA Ops:
  0.6 70.8 %sum_all.1 = (bf16[256,512]{1,0:T(8,128)(2,1)S(1)}, bf16[192,1536]{1,0:T(8,128)(2,1)S(1)}, f32[128,256]{1,0:T(8,128)S(1)}, f32[96,768]{1,0:T(8,128)S(1)}) custom-call(bf16[512,256]{1,0:T(8,128)(2,1)} %lat_kv.1, bf16[512,768]{1,0:T(8,128)(2,1)} %lat_q.1, bf16[512,8192]{1,0:T(8,128)(2,1)} %grad_kv.1, bf16[512,6144]{1,0:T(8,128)(2,1)} %grad_q.1, ...), custom_call_target="tpu_custom_call" | custom-call | tf_op jit(solution)/shard_map/sum_all/pallas_call | solution.py:502
  71.4 4.7 %closing.1 = (bf16[128,256]{1,0:T(8,128)(2,1)}, f32[128,256]{1,0:T(8,128)}, bf16[96,768]{1,0:T(8,128)(2,1)}, f32[96,768]{1,0:T(8,128)}) custom-call(bf16[256,512]{1,0:T(8,128)(2,1)S(1)} %get-tuple-element.8.prep_k, bf16[192,1536]{1,0:T(8,128)(2,1)S(1)} %get-tuple-element.9.prep_q, f32[128,256]{1,0:T(8,128)S(1)} %get-tuple-element.10.new_k, ...), custom_call_target="tpu_custom_call" | custom-call | tf_op jit(solution)/shard_map/closing/pallas_call | solution.py:538

commit v6 on v5

--- a/solution.py
+++ b/solution.py
@@ -207,15 +207,16 @@
             pltpu.make_async_remote_copy(
                 src_ref=source,
                 dst_ref=target,
-                send_sem=send_sem.at[self.index, s],
+                send_sem=send_sem.at[self.index],
                 recv_sem=self.sem(s, stage) if stage < 4 else recv_sem.at[self.index, 12],
                 device_id=(ways[axis, step], core),
                 device_id_type=MESH,
             ).start()
 
         def sent(self):
-            for s in range(3):
-                take(run(self.parts[s], 0, 63), send_sem.at[self.index, s])
+            units, rows, width = (14, 432, 384) if self.index < 2 else (7, 288, 512)
+            many = gk.at[pl.ds(0, units), pl.ds(0, rows), pl.ds(0, width)]
+            take(many, send_sem.at[self.index])
 
         def far(self, s, half):
             part, got, axis = self.parts[s], self.ones[s], ORDERS[s][0]
@@ -525,7 +526,7 @@
             pltpu.SemaphoreType.DMA((6,)),
             pltpu.SemaphoreType.DMA((4,)),
             pltpu.SemaphoreType.DMA((5,)),
-            pltpu.SemaphoreType.DMA((4, 3)),
+            pltpu.SemaphoreType.DMA((4,)),
             pltpu.SemaphoreType.DMA((4, 13)),
             pltpu.SemaphoreType.DMA((4,)),
             pltpu.SemaphoreType.DMA((4, 2)),

time: 76.4 us -> 76.3 us (level)
  no operation moved by 1% of the time
where the time goes in v6:
time: 76.3 us; the launch traced here: 76.2 us
  Pallas kernels  75.4 us (99%)
  between operations  0.8 us (1%)
    pallas_call x1, Pallas kernels, per_device(): pl.pallas_call(kernel, out_shape=(pltpu.VMEM((2 * KV_ROWS, 2 * KV_COLS),...  70.7 us
    pallas_call x1, Pallas kernels, per_device(): pl.pallas_call(closing, out_shape=(jax.ShapeDtypeStruct((KV_ROWS, KV_COLS...  4.73 us

profile of v6, /device:TPU:1, one launch (start us, length us, event | category | flops | bytes accessed | tf_op | source)
XLA Modules:
  0.0 76.2 jit_solution(18054861276305125961)
XLA Ops:
  0.6 70.7 %sum_all.1 = (bf16[256,512]{1,0:T(8,128)(2,1)S(1)}, bf16[192,1536]{1,0:T(8,128)(2,1)S(1)}, f32[128,256]{1,0:T(8,128)S(1)}, f32[96,768]{1,0:T(8,128)S(1)}) custom-call(bf16[512,256]{1,0:T(8,128)(2,1)} %lat_kv.1, bf16[512,768]{1,0:T(8,128)(2,1)} %lat_q.1, bf16[512,8192]{1,0:T(8,128)(2,1)} %grad_kv.1, bf16[512,6144]{1,0:T(8,128)(2,1)} %grad_q.1, ...), custom_call_target="tpu_custom_call" | custom-call | tf_op jit(solution)/shard_map/sum_all/pallas_call | solution.py:503
  71.3 4.7 %closing.1 = (bf16[128,256]{1,0:T(8,128)(2,1)}, f32[128,256]{1,0:T(8,128)}, bf16[96,768]{1,0:T(8,128)(2,1)}, f32[96,768]{1,0:T(8,128)}) custom-call(bf16[256,512]{1,0:T(8,128)(2,1)S(1)} %get-tuple-element.8.prep_k, bf16[192,1536]{1,0:T(8,128)(2,1)S(1)} %get-tuple-element.9.prep_q, f32[128,256]{1,0:T(8,128)S(1)} %get-tuple-element.10.new_k, ...), custom_call_target="tpu_custom_call" | custom-call | tf_op jit(solution)/shard_map/closing/pallas_call | solution.py:539
